TPU v7x, 32 devices: a whole 2x2x4 slice. The times are simulated.
32 devices in a mesh: groups: 2 (over x), wide: 8 (over z, y), narrow: 2 (over core).
Axes of the slice: x: 2, y: 2, z: 4, core: 2. Of those that a mesh axis runs over, the one named last changes fastest.
Arguments:
- context_symbol_ids: int32 [2, 16, 16], P('narrow', 'groups'), parts along dimension 1, may hold values from 0 to 32767
- context_symbol_spans: int32 [2, 16], P('narrow', 'groups'), parts along dimension 1, may hold values from 1 to 16, as said below
- symbol_vector_lookup: bfloat16 [4096, 32768], P('wide'), may hold values from -6 to 6
- opening_lagged_blend: float32 [4096], replicated, may hold values from 0 to 1
- lagged_blend_weights: float32 [3, 4096], replicated, may hold values from 0 to 1
- blending_left_operand: bfloat16 [4096, 192], replicated, may hold values from -0.09375 to 0.09375
- blending_right_operands: bfloat16 [3, 64, 4096], replicated, may hold values from -0.375 to 0.375
- fixed_fading_scores: float32 [4096], P('wide'), may hold values from -6 to -1
- fading_left_operand: bfloat16 [4096, 128], replicated, may hold values from -0.09375 to 0.09375
- fading_right_operand: bfloat16 [128, 4096], P(None, 'wide'), may hold values from -0.5 to 0.5
- address_projector: bfloat16 [4096, 4096], P('wide'), may hold values from -0.09375 to 0.09375
- payload_projector: bfloat16 [4096, 4096], P('wide'), may hold values from -0.09375 to 0.09375
- present_symbol_reward: float32 [64, 64], replicated, may hold values from -1 to 1
- cluster_scaling_weight: float32 [4096], replicated, may hold values from 0.5 to 1.5
- cluster_scaling_offset: float32 [4096], replicated, may hold values from -3 to 3
- generated_acceptance: bfloat16 [2, 16, 4, 4096], P(None, ('groups', 'wide'), None, 'narrow'), parts along dimension 1, may hold values from -6 to 6
- generated_addresses: bfloat16 [2, 16, 4, 4096], P(None, ('groups', 'wide'), None, 'narrow'), parts along dimension 1, may hold values from -6 to 6
- generated_payloads: bfloat16 [2, 16, 4, 4096], P(None, ('groups', 'wide'), None, 'narrow'), parts along dimension 1, may hold values from -6 to 6
- generated_fading_scores: bfloat16 [2, 16, 4, 4096], P(None, ('groups', 'wide'), None, 'narrow'), parts along dimension 1, may hold values from -6 to -1
- generated_valve_scores: bfloat16 [2, 16, 4, 4096], P(None, ('groups', 'wide'), None, 'narrow'), parts along dimension 1, may hold values from -6 to 6
Outputs:
- dec_out: bfloat16 [2, 16, 4, 4096], P(None, ('groups', 'wide'), None, 'narrow'), parts along dimension 1
There are 2 independent parts, one for each index of `groups`. A program takes and returns all parts, laid end to end along the dimension named above; an argument that names none is the same for every part. Nothing has to cross between parts.
Inputs may be any that keep to these rules, and one draw needn't show every extreme that they name: `context_symbol_spans`: positions at or past a prompt's length are padding. In every draw one of the 2 banks, chosen by the draw, holds only prompts of exactly 16 tokens, and every other bank holds at least one prompt of 16 tokens.
All inputs are finite; a program needn't handle non-finite values.
Results may differ from a plain program's by a relative error of at most 0.0095.
Values may be sent and summed in bfloat16 or wider, within the bound.
A program may use at most 128 MiB of HBM per device.

v0:
```python
import jax
import jax.numpy as jnp
from jax import lax
from jax.sharding import PartitionSpec as P

norm_eps = 0.00064


def mix_project(
    embedded,
    opening_lagged_blend,
    lagged_blend_weights,
    blending_left_operand,
    blending_right_operands,
    fixed_fading_scores,
    fading_left_operand,
    fading_right_operand,
    address_projector,
    payload_projector,
):
    features = embedded.shape[2]
    previous = jnp.pad(embedded, ((0, 0), (1, 0), (0, 0)))[:, :-1, :]
    current = embedded.reshape(-1, features).astype(jnp.float32)
    difference = previous.reshape(-1, features).astype(jnp.float32) - current
    mixed_in = (current + difference * opening_lagged_blend).astype(jnp.bfloat16)
    hidden = jnp.tanh(
        jnp.dot(mixed_in, blending_left_operand, preferred_element_type=jnp.float32)
    ).astype(jnp.bfloat16)
    rank_size = blending_right_operands.shape[1]
    branches = []
    for branch in range(3):
        shift_term = jnp.dot(
            hidden[:, branch * rank_size : (branch + 1) * rank_size],
            blending_right_operands[branch],
            preferred_element_type=jnp.float32,
        )
        branches.append(
            (current + difference * (lagged_blend_weights[branch] + shift_term)).astype(
                jnp.bfloat16
            )
        )
    decay_hidden = jnp.tanh(
        jnp.dot(branches[0], fading_left_operand, preferred_element_type=jnp.float32)
    ).astype(jnp.bfloat16)
    decay_log = fixed_fading_scores + jnp.dot(
        decay_hidden, fading_right_operand, preferred_element_type=jnp.float32
    )
    key_proj = jnp.dot(branches[1], address_projector.T, preferred_element_type=jnp.float32).astype(
        jnp.bfloat16
    )
    value_proj = jnp.dot(
        branches[2], payload_projector.T, preferred_element_type=jnp.float32
    ).astype(jnp.bfloat16)
    return (key_proj, value_proj, decay_log)


def final_states(key_proj, value_proj, decay_log, lengths, attender_width):
    bank_rows, length, columns = key_proj.shape
    attender_ordinal = columns // attender_width
    decay_rates = jnp.exp(decay_log)
    places = lax.broadcasted_iota(jnp.int32, (bank_rows, length), 1)
    live_mask = (places < lengths[:, None])[:, :, None]
    running = jnp.cumsum(jnp.where(live_mask, decay_rates, 0.0), axis=1)
    remaining = running[:, -1:, :] - running
    weights = jnp.where(live_mask, jnp.exp(-remaining), 0.0)
    weighted = (key_proj.astype(jnp.float32) * weights).reshape(
        bank_rows, length, attender_ordinal, attender_width
    )
    plain_values = value_proj.astype(jnp.float32).reshape(
        bank_rows, length, attender_ordinal, attender_width
    )
    return jnp.einsum("rlhi,rlhj->rhij", weighted, plain_values, precision=lax.Precision.HIGHEST)


def generation_iterations(
    recurrent_memories,
    acceptance_lines,
    address_source,
    payload_source,
    fading_source,
    valve_source,
    shard_reward,
    shard_scaling_weight,
    shard_scaling_offset,
):
    attender_ordinal = recurrent_memories.shape[-3]
    attender_width = recurrent_memories.shape[-1]
    leading = acceptance_lines.shape[:-2]
    step_count = acceptance_lines.shape[-2]
    split_shape = leading + (step_count, attender_ordinal, attender_width)
    receptance = acceptance_lines.astype(jnp.float32).reshape(split_shape)
    key_split = address_source.astype(jnp.float32).reshape(split_shape)
    valued = payload_source.astype(jnp.float32).reshape(split_shape)
    factors = jnp.exp(-jnp.exp(fading_source.astype(jnp.float32))).reshape(split_shape)
    results = []
    for position in range(step_count):
        present_acceptance = receptance[..., position, :, :]
        present_address = key_split[..., position, :, :]
        present_payload = valued[..., position, :, :]
        immediate_summand = (
            jnp.sum(present_acceptance * shard_reward * present_address, axis=-1, keepdims=True)
            * present_payload
        )
        carried = jnp.einsum(
            "...hi,...hij->...hj",
            present_acceptance,
            recurrent_memories,
            precision=lax.Precision.HIGHEST,
        )
        results.append(carried + immediate_summand)
        if position + 1 < step_count:
            recurrent_memories = (
                factors[..., position, :, :][..., :, None] * recurrent_memories
                + present_address[..., :, None] * present_payload[..., None, :]
            )
    mixed_out = jnp.stack(results, axis=-3)
    average = jnp.mean(mixed_out, axis=-1, keepdims=True)
    centred = mixed_out - average
    spread = jnp.mean(centred * centred, axis=-1, keepdims=True)
    normed = (centred * lax.rsqrt(spread + norm_eps)).reshape(
        leading + (step_count, attender_ordinal * attender_width)
    )
    return (
        (normed * shard_scaling_weight + shard_scaling_offset)
        * jax.nn.silu(valve_source.astype(jnp.float32))
    ).astype(jnp.bfloat16)


def per_device(
    context_symbol_ids,
    context_symbol_spans,
    symbol_vector_lookup,
    opening_lagged_blend,
    lagged_blend_weights,
    blending_left_operand,
    blending_right_operands,
    fixed_fading_scores,
    fading_left_operand,
    fading_right_operand,
    address_projector,
    payload_projector,
    present_symbol_reward,
    cluster_scaling_weight,
    cluster_scaling_offset,
    generated_acceptance,
    generated_addresses,
    generated_payloads,
    generated_fading_scores,
    generated_valve_scores,
):
    bank_rows = context_symbol_ids.shape[1]
    length = context_symbol_ids.shape[2]
    columns = symbol_vector_lookup.shape[0]
    attender_width = present_symbol_reward.shape[1]
    head_local = columns // attender_width
    lengths = context_symbol_spans.reshape(-1)
    picked = jnp.take(symbol_vector_lookup, context_symbol_ids.reshape(-1), axis=1)
    gathered = lax.all_gather(picked, "wide", axis=0, tiled=True).T
    features = gathered.shape[1]
    block_rows = bank_rows
    while block_rows % 2 == 0 and block_rows * length > 1024:
        block_rows = block_rows // 2
    blocks = gathered.reshape(bank_rows // block_rows, block_rows, length, features)
    length_blocks = lengths.reshape(bank_rows // block_rows, block_rows)

    def one_block(block_item):
        key_proj, value_proj, decay_log = mix_project(
            block_item[0],
            opening_lagged_blend,
            lagged_blend_weights,
            blending_left_operand,
            blending_right_operands,
            fixed_fading_scores,
            fading_left_operand,
            fading_right_operand,
            address_projector,
            payload_projector,
        )
        block_shape = (block_rows, length, columns)
        return final_states(
            key_proj.reshape(block_shape),
            value_proj.reshape(block_shape),
            decay_log.reshape(block_shape),
            block_item[1],
            attender_width,
        )

    recurrent_memories = lax.map(one_block, (blocks, length_blocks)).reshape(
        bank_rows, head_local, attender_width, attender_width
    )
    handed = lax.all_to_all(
        lax.all_to_all(
            recurrent_memories.reshape(1, bank_rows, head_local, attender_width * attender_width),
            "wide",
            split_axis=1,
            concat_axis=2,
            tiled=True,
        ),
        "narrow",
        split_axis=2,
        concat_axis=0,
        tiled=True,
    )
    generated_by_attender = handed.shape[2]
    leading_attender_offset = lax.axis_index("narrow") * generated_by_attender
    shard_reward = lax.dynamic_slice_in_dim(
        present_symbol_reward, leading_attender_offset, generated_by_attender, 0
    )
    shard_scaling_weight = lax.dynamic_slice_in_dim(
        cluster_scaling_weight,
        leading_attender_offset * attender_width,
        generated_by_attender * attender_width,
        0,
    )
    shard_scaling_offset = lax.dynamic_slice_in_dim(
        cluster_scaling_offset,
        leading_attender_offset * attender_width,
        generated_by_attender * attender_width,
        0,
    )
    result = generation_iterations(
        handed.reshape(handed.shape[:3] + (attender_width, attender_width)),
        generated_acceptance,
        generated_addresses,
        generated_payloads,
        generated_fading_scores,
        generated_valve_scores,
        shard_reward,
        shard_scaling_weight,
        shard_scaling_offset,
    )
    return result


def solution(mesh):
    placed = (
        P("narrow", "groups", None),
        P("narrow", "groups"),
        P("wide", None),
        P(),
        P(),
        P(),
        P(),
        P("wide"),
        P(),
        P(None, "wide"),
        P("wide", None),
        P("wide", None),
        P(),
        P(),
        P(),
        P(None, ("groups", "wide"), None, "narrow"),
        P(None, ("groups", "wide"), None, "narrow"),
        P(None, ("groups", "wide"), None, "narrow"),
        P(None, ("groups", "wide"), None, "narrow"),
        P(None, ("groups", "wide"), None, "narrow"),
    )
    return jax.shard_map(
        per_device,
        mesh=mesh,
        in_specs=placed,
        out_specs=P(None, ("groups", "wide"), None, "narrow"),
        check_vma=False,
    )
```

profile of v0, /device:TPU:1, one launch (start us, length us, event | category | flops | bytes accessed | tf_op | source)
XLA Modules:
  0.0 181.2 jit_solution(2919527989202924769)
XLA Ops:
  6.5 0.9 reshape.534
  7.4 0.8 reshape.533
  8.2 44.0 %copy.70 = bf16[512,32768]{0,1:T(8,128)(2,1)} copy(bf16[512,32768]{1,0:T(8,128)(2,1)} %param.22) | data formatting | bytes 67108864 | tf_op args[2]
  52.2 2.0 %gather_fusion = bf16[128,512]{1,0:T(8,128)(2,1)S(1)} fusion(bf16[512,32768]{0,1:T(8,128)(2,1)} %copy.70, s32[1024]{0:T(1024)S(1)} %pad_clamp_fusion), kind=kCustom, calls=%fused_computation | custom fusion | bytes 262656 | tf_op jit(solution)/shard_map/jit(_take)/gather | solution.py:157
  54.2 0.7 select_bitcast_fusion
  55.1 39.2 %all-gather.2.cloned.1.call-done = bf16[4096,128]{0,1:T(8,128)(2,1)} async-done(((bf16[512,128]{0,1:T(8,128)(2,1)}), bf16[4096,128]{0,1:T(8,128)(2,1)}) %all-gather.2.cloned.1.call-update) | async-done | bytes 1048592 | tf_op jit(solution)/shard_map/all_gather | solution.py:158
  94.3 1.6 pad_slice_fusion
  95.9 0.7 fusion.20
  96.6 0.3 copy-done.4
  96.9 2.7 %fusion.22 = bf16[128,128]{1,0:T(8,128)(2,1)S(1)} fusion(bf16[4096,128]{1,0:T(8,128)(2,1)} %param.28, bf16[128,4096]{1,0:T(8,128)(2,1)} %bitcast.181, bf16[4096,128]{0,1:T(8,128)(2,1)S(1)} %copy-done.3, f32[4096]{0:T(1024)S(1)} %bitcast.199, bf16[3,64,4096]{2,1,0:T(8,128)(2,1)} %param.26, bf16[128,192]{0,1:T(8,128)(2,1)S(1)} %fusion.20), kind=kOutput, calls=%fused_computation.35 | convolution fusion | flops 205012992 | bytes 3735552 | tf_op jit(solution)/shard_map/while/body/eval_jaxpr/dot_general | solution.py:43
  99.6 0.2 fusion.18
  99.8 0.2 fusion.68
  100.0 0.1 reduce_window_sum.15
  100.2 4.7 %convolution_convert_fusion = bf16[128,512]{1,0:T(8,128)(2,1)S(1)} fusion(bf16[512,4096]{1,0:T(8,128)(2,1)} %param.31, bf16[128,4096]{1,0:T(8,128)(2,1)} %bitcast.182, bf16[4096,128]{0,1:T(8,128)(2,1)S(1)} %copy-done.3, f32[4096]{0:T(1024)S(1)} %bitcast.198, bf16[3,64,4096]{2,1,0:T(8,128)(2,1)} %param.26, bf16[128,192]{0,1:T(8,128)(2,1)S(1)} %fusion.20), kind=kOutput, calls=%fused_computation.29 | convolution fusion | flops 607715328 | bytes 6979584 | tf_op jit(solution)/shard_map/while/body/eval_jaxpr/dot_general | solution.py:51
  104.9 0.2 reshape.535
  105.1 4.7 %fusion.19 = f32[128,512]{1,0:T(8,128)S(1)} fusion(bf16[512,4096]{1,0:T(8,128)(2,1)} %param.30, bf16[128,4096]{1,0:T(8,128)(2,1)} %bitcast.183, bf16[4096,128]{0,1:T(8,128)(2,1)S(1)} %copy-done.3, f32[4096]{0:T(1024)S(1)} %bitcast.197, bf16[3,64,4096]{2,1,0:T(8,128)(2,1)} %param.26, bf16[128,192]{0,1:T(8,128)(2,1)S(1)} %fusion.20), kind=kOutput, calls=%fused_computation.31 | convolution fusion | flops 607780864 | bytes 7110656 | tf_op jit(solution)/shard_map/while/body/eval_jaxpr/dot_general | solution.py:48
  109.8 0.1 reshape.549
  109.9 3.3 %fusion.56 = f32[8,8,64,64]{3,2,1,0:T(8,128)} fusion(f32[8,16,8,64]{3,2,1,0:T(8,128)S(1)} %reshape.549, f32[8,16,8,64]{3,2,0,1:T(8,128)S(1)} %reduce_window_sum.15, bf16[8,16,8,64]{3,2,1,0:T(8,128)(2,1)S(1)} %reshape.535, f32[8,8,64]{2,1,0:T(8,128)S(1)} %sub.51, pred[8,16]{1,0:T(8,128)(4,1)S(1)} %copy.71), kind=kOutput, calls=%fused_computation.66 | convolution fusion | flops 50593792 | bytes 1720448 | tf_op jit(solution)/shard_map/while/body/eval_jaxpr/rlhi,rlhj->rhij/dot_general | solution.py:72
  113.2 2.9 %reshape_reshape.3 = f32[1,8,8,4096]{3,2,1,0:T(8,128)} reshape(f32[8,8,64,64]{3,2,1,0:T(8,128)} %fusion.56) | data formatting | bytes 2097152 | tf_op jit(solution)/shard_map/reshape;reshape | solution.py:193
  116.2 5.4 %all-to-all-start = ((f32[1,8,8,4096]{3,2,0,1:T(8,128)}), f32[1,8,8,4096]{3,2,0,1:T(8,128)S(1)}, u32[]{:S(2)}, u32[]{:S(2)}) async-start(f32[1,8,8,4096]{3,2,0,1:T(8,128)} %bitcast.13), calls=%async_computation | async-start | bytes 2097152 | tf_op jit(solution)/shard_map/all_to_all | solution.py:192
  121.7 0.1 reshape.544
  122.3 23.9 %all-to-all-done = f32[1,8,8,4096]{3,2,0,1:T(8,128)S(1)} async-done(((f32[1,8,8,4096]{3,2,0,1:T(8,128)}), f32[1,8,8,4096]{3,2,0,1:T(8,128)S(1)}, u32[]{:S(2)}, u32[]{:S(2)}) %all-to-all-start) | async-done | bytes 1048608 | tf_op jit(solution)/shard_map/all_to_all | solution.py:192
  146.2 1.1 copy.77
  147.2 6.6 %all_to_all.21 = f32[1,1,64,4096]{3,1,0,2:T(1,128)S(1)} all-to-all(f32[1,1,64,4096]{3,1,0,2:T(1,128)S(1)} %copy.77), channel_id=1, replica_groups=mesh['groups'=2,'wide'=8,'narrow'=2] {'narrow'}, dimensions={2} | all-to-all | bytes 2097152 | tf_op jit(solution)/shard_map/all_to_all | solution.py:191
  153.8 2.6 %reduce.6 = f32[64,4096]{1,0:T(8,128)S(1)} reduce(f32[1,1,64,4096]{3,1,0,2:T(1,128)S(1)} %all_to_all.21, f32[]{:T(128)} %constant.68), dimensions={0,1}, to_apply=%all_to_all.8.reduce_sub_computation | reduce | bytes 2097156 | tf_op jit(solution)/shard_map/all_to_all | solution.py:191
  156.4 2.2 %reshape.536 = f32[2,32,64,64]{3,2,1,0:T(8,128)} reshape(f32[64,4096]{1,0:T(8,128)S(1)} %reduce.6) | data formatting | bytes 2097152 | tf_op jit(solution)/shard_map/reshape.34
  158.6 2.8 %fusion.99 = f32[2,32,1,64]{3,2,1,0:T(1,128)S(1)} fusion(f32[2,32,64,64]{3,2,1,0:T(8,128)} %reshape.536, bf16[2,32,64,1]{2,1,0,3:T(8,128)(2,1)S(1)} %get-tuple-element.61), kind=kOutput, calls=%fused_computation.127 | convolution fusion | flops 3145728 | bytes 1073152 | tf_op jit(solution)/shard_map/...hi,...hij->...hj/dot_general | solution.py:104
  161.4 2.0 %fusion.15 = f32[2,32,1,64]{3,2,1,0:T(1,128)S(1)} fusion(f32[2,32,64,64]{3,2,1,0:T(8,128)S(1)} %copy-done.2, f32[2,32,64]{2,1,0:T(8,128)S(1)} %get-tuple-element.70, f32[2,32,64]{2,1,0:T(8,128)S(1)} %get-tuple-element.54, f32[2,32,64]{2,1,0:T(8,128)S(1)} %get-tuple-element.37, bf16[2,32,64,1]{2,1,0,3:T(8,128)(2,1)S(1)} %get-tuple-element.64), kind=kOutput, calls=%fused_computation.23 | convolution fusion | flops 3932160 | bytes 1122304 | tf_op jit(solution)/shard_map/...hi,...hij->...hj/dot_general | solution.py:104
  163.4 3.5 %fusion.17 = f32[2,32,1,64]{3,2,1,0:T(1,128)S(1)} fusion(f32[2,32,64,64]{3,2,1,0:T(8,128)S(1)} %copy-done.2, f32[2,32,64]{2,1,0:T(8,128)S(1)} %get-tuple-element.68, f32[2,32,64]{2,1,0:T(8,128)S(1)} %get-tuple-element.56, f32[2,32,64]{2,1,0:T(8,128)S(1)} %get-tuple-element.52, f32[2,32,64]{2,1,0:T(8,128)S(1)} %get-tuple-element.70, ...), kind=kOutput, calls=%fused_computation.26 | convolution fusion | flops 4718592 | bytes 1171456 | tf_op jit(solution)/shard_map/...hi,...hij->...hj/dot_general | solution.py:104
  167.0 5.3 %fusion.11 = f32[2,32,1,64]{3,2,1,0:T(1,128)S(1)} fusion(f32[2,32,64,64]{3,2,1,0:T(8,128)S(1)} %copy-done.2, f32[2,32,64]{2,1,0:T(8,128)S(1)} %get-tuple-element.69, f32[2,32,64]{2,1,0:T(8,128)S(1)} %get-tuple-element.57, f32[2,32,64]{2,1,0:T(8,128)S(1)} %get-tuple-element.38, f32[2,32,64]{2,1,0:T(8,128)S(1)} %get-tuple-element.68, ...), kind=kOutput, calls=%fused_computation.17 | convolution fusion | flops 5505024 | bytes 1220608 | tf_op jit(solution)/shard_map/...hi,...hij->...hj/dot_general | solution.py:104
  172.6 0.2 multiply_reduce_fusion
  173.6 0.7 fusion.81
  (69 shorter events, 1.9 us)
Async XLA Ops:
  6.5 89.3 %copy-start = (bf16[4096,192]{0,1:T(8,128)(2,1)S(1)}, bf16[4096,192]{0,1:T(8,128)(2,1)}, u32[]{:S(2)}) copy-start(bf16[4096,192]{0,1:T(8,128)(2,1)} %param.25) | copy-start | bytes 4718596
  6.5 87.7 %all-gather.2.cloned.1.call-start = ((), (), s32[]{:S(2)}) async-start(), calls=%async_computation.2 | async-start | bytes 1179648 | tf_op jit(solution)/shard_map/all_gather | solution.py:158
  8.2 46.7 %copy-start.14 = (s32[1,8]{1,0:T(1,128)S(1)}, s32[1,8]{1,0:T(1,128)}, u32[]{:S(2)}) copy-start(s32[1,8]{1,0:T(1,128)} %param.21) | copy-start | bytes 100
  8.2 46.9 %copy-start.6 = (f32[3,4096]{1,0:T(4,128)S(1)}, f32[3,4096]{1,0:T(4,128)}, u32[]{:S(2)}) copy-start(f32[3,4096]{1,0:T(4,128)} %param.24) | copy-start | bytes 147460
  52.2 43.7 %copy-start.15 = (f32[4096]{0:T(1024)S(1)}, f32[4096]{0:T(1024)}, u32[]{:S(2)}) copy-start(f32[4096]{0:T(1024)} %param.23) | copy-start | bytes 49156
  94.3 1.6 copy-start.3
  95.9 1.0 copy-start.4
  96.9 2.7 %copy-start.5 = (bf16[128,512]{1,0:T(8,128)(2,1)S(1)}, bf16[128,512]{1,0:T(8,128)(2,1)}, u32[]{:S(2)}) copy-start(bf16[128,512]{1,0:T(8,128)(2,1)} %param.29) | copy-start | bytes 393220
  96.9 2.7 %copy-start.13 = (f32[512]{0:T(512)S(1)}, f32[512]{0:T(512)}, u32[]{:S(2)}) copy-start(f32[512]{0:T(512)} %param.27) | copy-start | bytes 6148
  113.2 8.3 %copy-start.7 = (bf16[2,1,4,2048]{3,2,1,0:T(4,128)(2,1)S(1)}, bf16[2,1,4,2048]{3,2,1,0:T(4,128)(2,1)}, u32[]{:S(2)}) copy-start(bf16[2,1,4,2048]{3,2,1,0:T(4,128)(2,1)} %param.37) | copy-start | bytes 98308
  113.2 8.4 %copy-start.8 = (bf16[2,1,4,2048]{3,2,1,0:T(4,128)(2,1)S(1)}, bf16[2,1,4,2048]{3,2,1,0:T(4,128)(2,1)}, u32[]{:S(2)}) copy-start(bf16[2,1,4,2048]{3,2,1,0:T(4,128)(2,1)} %param.38) | copy-start | bytes 98308
  113.2 8.6 %copy-start.9 = (bf16[2,1,4,2048]{3,2,1,0:T(4,128)(2,1)S(1)}, bf16[2,1,4,2048]{3,2,1,0:T(4,128)(2,1)}, u32[]{:S(2)}) copy-start(bf16[2,1,4,2048]{3,2,1,0:T(4,128)(2,1)} %param.36) | copy-start | bytes 98308
  116.1 5.8 %copy-start.10 = (bf16[2,1,4,2048]{3,2,1,0:T(4,128)(2,1)S(1)}, bf16[2,1,4,2048]{3,2,1,0:T(4,128)(2,1)}, u32[]{:S(2)}) copy-start(bf16[2,1,4,2048]{3,2,1,0:T(4,128)(2,1)} %param.35) | copy-start | bytes 98308
  116.1 5.9 %copy-start.12 = (f32[64,64]{1,0:T(8,128)S(1)}, f32[64,64]{1,0:T(8,128)}, u32[]{:S(2)}) copy-start(f32[64,64]{1,0:T(8,128)} %param.32) | copy-start | bytes 49156
  116.2 30.0 %all-to-all-start = ((f32[1,8,8,4096]{3,2,0,1:T(8,128)}), f32[1,8,8,4096]{3,2,0,1:T(8,128)S(1)}, u32[]{:S(2)}, u32[]{:S(2)}) async-start(f32[1,8,8,4096]{3,2,0,1:T(8,128)} %bitcast.13), calls=%async_computation | async-start | bytes 2097152 | tf_op jit(solution)/shard_map/all_to_all | solution.py:192
  158.6 2.8 %copy-start.2 = (f32[2,32,64,64]{3,2,1,0:T(8,128)S(1)}, f32[2,32,64,64]{3,2,1,0:T(8,128)}, u32[]{:S(2)}) copy-start(f32[2,32,64,64]{3,2,1,0:T(8,128)} %reshape.536) | copy-start | bytes 3145732
  166.9 6.7 %copy-start.11 = (bf16[2,1,4,2048]{3,2,1,0:T(4,128)(2,1)S(1)}, bf16[2,1,4,2048]{3,2,1,0:T(4,128)(2,1)}, u32[]{:S(2)}) copy-start(bf16[2,1,4,2048]{3,2,1,0:T(4,128)(2,1)} %param.39) | copy-start | bytes 98308
  167.0 6.7 %dynamic-slice-start = ((f32[4096]{0:T(1024)}, s32[]{:T(128)}), f32[2048]{0:T(1024)S(1)}, s32[]{:S(2)}) async-start(f32[4096]{0:T(1024)} %param.33, s32[]{:T(128)} %select_n.43), calls=%async_computation.3 | async-start | bytes 16896 | tf_op jit(solution)/shard_map/dynamic_slice | solution.py:209
  167.0 6.6 %dynamic-slice-start.1 = ((f32[4096]{0:T(1024)}, s32[]{:T(128)}), f32[2048]{0:T(1024)S(1)}, s32[]{:S(2)}) async-start(f32[4096]{0:T(1024)} %param.34, s32[]{:T(128)} %select_n.43), calls=%async_computation.4 | async-start | bytes 16896 | tf_op jit(solution)/shard_map/dynamic_slice | solution.py:215
  167.0 7.4 %copy-start.1 = (bf16[4096,192]{0,1:T(8,128)(2,1)S(1)}, bf16[4096,192]{0,1:T(8,128)(2,1)}, u32[]{:S(2)}) copy-start(bf16[4096,192]{0,1:T(8,128)(2,1)} %param.25) | copy-start | bytes 4718596
Sparse Core Ops, SparseCore 0:
  55.1 39.1 all-gather.1
where the time goes:
time: 183 us; the launch traced here: 181 us
  waiting for transfers between devices  63.1 us (34%)
  local copies, waits for them, and re-layouts  57.6 us (31%)
  matrix products  29.9 us (16%)
  between operations  13.8 us (8%)
  blocking collectives  6.56 us (4%)
  starting transfers between devices  5.37 us (3%)
  other arithmetic  4.89 us (3%)
    unnamed x33, local copies, waits for them, and re-layouts  44.4 us
    all_gather x1, waiting for transfers between devices, per_device(): gathered = lax.all_gather(picked, 'wide', axis=0, tiled=True).T  39.2 us
    all_to_all x1, waiting for transfers between devices, per_device(): lax.all_to_all(recurrent_memories.reshape(1, bank_rows, head_local, atten...  23.9 us
    dot_general x4, matrix products, generation_iterations(): jnp.einsum('...hi,...hij->...hj', present_acceptance, recurrent_memories,...  13.7 us
    all_to_all x1, blocking collectives, per_device(): lax.all_to_all(lax.all_to_all(recurrent_memories.reshape(1, bank_rows, he...  6.56 us
    all_to_all x1, starting transfers between devices, per_device(): lax.all_to_all(recurrent_memories.reshape(1, bank_rows, head_local, atten...  5.37 us
    dot_general x1, matrix products, mix_project(): jnp.dot(branches[1], address_projector.T, preferred_element_type=jnp.floa...  4.66 us
    dot_general x1, matrix products, mix_project(): jnp.dot(branches[2], payload_projector.T, preferred_element_type=jnp.floa...  4.65 us
  transfers between devices with their start and end apart: 2, of which 2 were waited for; matrix products, arithmetic and copies ran while one was open for 0% of the time, Pallas kernels for 0%

commit v1 on v0

--- a/solution.py
+++ b/solution.py
@@ -1,9 +1,14 @@
+import functools
+
 import jax
 import jax.numpy as jnp
 from jax import lax
+from jax.experimental import pallas as pl
+from jax.experimental.pallas import tpu as pltpu
 from jax.sharding import PartitionSpec as P
 
 norm_eps = 0.00064
+lane_count = 128
 
 
 def mix_project(
@@ -126,6 +131,616 @@
     ).astype(jnp.bfloat16)
 
 
+def gather_body(ids_ref, table_ref, out_ref, strips, sems):
+    rows, length = ids_ref.shape[1], ids_ref.shape[2]
+    lanes = strips.shape[2] // length
+
+    def strip(row, place):
+        tile = lax.div(ids_ref[0, row, place], lanes)
+        return pltpu.make_async_copy(
+            table_ref.at[:, pl.ds(pl.multiple_of(tile * lanes, lanes), lanes)],
+            strips.at[row, :, pl.ds(place * lanes, lanes)],
+            sems.at[row, place],
+        )
+
+    def start(row, carry):
+        for place in range(length):
+            strip(row, place).start()
+        return carry
+
+    lax.fori_loop(0, rows, start, 0)
+    places = lax.broadcasted_iota(jnp.int32, (length, lanes), 0)
+    columns = lax.broadcasted_iota(jnp.int32, (length, lanes), 1)
+
+    def pick(row, carry):
+        wanted = jnp.zeros((length, lanes), jnp.int32)
+        for place in range(length):
+            wanted = jnp.where(places == place, lax.rem(ids_ref[0, row, place], lanes), wanted)
+        hit = jnp.where(columns == wanted, 1.0, 0.0)
+        chosen = jnp.concatenate(
+            [jnp.where(places == place, hit, 0.0) for place in range(length)], axis=1
+        ).astype(jnp.bfloat16)
+        for place in range(length):
+            strip(row, place).wait()
+        found = lax.dot_general(
+            chosen, strips[row], (((1,), (1,)), ((), ())), preferred_element_type=jnp.float32
+        )
+        out_ref[pl.ds(pl.multiple_of(row * length, length), length), :] = found.astype(jnp.bfloat16)
+        return carry
+
+    lax.fori_loop(0, rows, pick, 0)
+
+
+def gather_tokens(ids, table):
+    rows, length = ids.shape[1], ids.shape[2]
+    columns = table.shape[0]
+    return pl.pallas_call(
+        gather_body,
+        out_shape=jax.ShapeDtypeStruct((rows * length, columns), jnp.bfloat16),
+        in_specs=[
+            pl.BlockSpec(memory_space=pltpu.SMEM),
+            pl.BlockSpec(memory_space=pl.ANY),
+        ],
+        out_specs=pl.BlockSpec(memory_space=pltpu.VMEM),
+        scratch_shapes=[
+            pltpu.VMEM((rows, columns, length * lane_count), jnp.bfloat16),
+            pltpu.SemaphoreType.DMA((rows, length)),
+        ],
+        compiler_params=pltpu.CompilerParams(vmem_limit_bytes=40 * 2**20),
+        name="pick_tokens",
+    )(ids, table)
+
+
+def segment_sums(rows, ones):
+    width = ones.shape[0]
+    high = rows.astype(jnp.bfloat16)
+    low = (rows - high.astype(jnp.float32)).astype(jnp.bfloat16)
+    parts = []
+    for begin in range(0, rows.shape[1], width):
+        stop = begin + width
+        parts.append(
+            jnp.dot(high[:, begin:stop], ones, preferred_element_type=jnp.float32)
+            + jnp.dot(low[:, begin:stop], ones, preferred_element_type=jnp.float32)
+        )
+    return jnp.concatenate(parts, axis=1)
+
+
+def mixing_body(
+    wide,
+    narrow,
+    spans_ref,
+    local_ref,
+    opening_ref,
+    blends_ref,
+    left_hbm,
+    right_hbm,
+    fixed_ref,
+    fading_left_hbm,
+    fading_right_ref,
+    address_hbm,
+    payload_hbm,
+    reward_ref,
+    scaling_ref,
+    offset_ref,
+    r_ref,
+    k_ref,
+    v_ref,
+    w_ref,
+    g_ref,
+    out_ref,
+    held,
+    left,
+    right,
+    fading_left,
+    address,
+    payload,
+    hidden_sum,
+    key_sum,
+    value_sum,
+    decay_sum,
+    pairs,
+    own_part,
+    r_send,
+    r_recv,
+    y_send,
+    y_recv,
+    weight_sems,
+    ring_send,
+    ring_recv,
+    r_send_sems,
+    r_recv_sems,
+    y_send_sems,
+    y_recv_sems,
+    self_sems,
+):
+    w_me = lax.axis_index("wide")
+    n_me = lax.axis_index("narrow")
+    tokens, columns = local_ref.shape
+    bank_rows = spans_ref.shape[1]
+    length = tokens // bank_rows
+    features = opening_ref.shape[1]
+    head = reward_ref.shape[1]
+    banks, steps, generated = r_ref.shape
+    share = wide // narrow
+    half_owner = lax.div(w_me, share)
+    place_in_half = lax.rem(w_me, share)
+
+    barrier = pltpu.get_barrier_semaphore()
+    for other in range(1, wide * narrow):
+        flat = lax.rem(w_me * narrow + n_me + other, wide * narrow)
+        pl.semaphore_signal(
+            barrier,
+            inc=1,
+            device_id={"wide": lax.div(flat, narrow), "narrow": lax.rem(flat, narrow)},
+            device_id_type=pl.DeviceIdType.MESH,
+        )
+
+    loads = [
+        pltpu.make_async_copy(source, target, weight_sems.at[number])
+        for number, (source, target) in enumerate(
+            [
+                (left_hbm, left),
+                (right_hbm, right),
+                (fading_left_hbm, fading_left),
+                (address_hbm, address),
+                (payload_hbm, payload),
+            ]
+        )
+    ]
+    for load in loads:
+        load.start()
+
+    held[w_me] = local_ref[...]
+
+    def index_at(position):
+        return jnp.where(position < wide // 2, 2 * position, 2 * (wide - 1 - position) + 1)
+
+    position = jnp.where(
+        lax.rem(w_me, 2) == 0, lax.div(w_me, 2), wide - 1 - lax.div(w_me, 2)
+    )
+    targets = (
+        index_at(lax.rem(position + 1, wide)),
+        index_at(lax.rem(position + wide - 1, wide)),
+    )
+    half = tokens // 2
+    chunk_rows = length
+    chunks = half // chunk_rows
+
+    def owner_of(direction, step):
+        back = wide - step if direction == 0 else step
+        return index_at(lax.rem(position + back, wide))
+
+    def ring_copy(direction, step, chunk):
+        piece = held.at[
+            owner_of(direction, step), pl.ds(direction * half + chunk * chunk_rows, chunk_rows)
+        ]
+        return pltpu.make_async_remote_copy(
+            src_ref=piece,
+            dst_ref=piece,
+            send_sem=ring_send.at[direction, step, chunk],
+            recv_sem=ring_recv.at[direction, step, chunk],
+            device_id={"wide": targets[direction]},
+            device_id_type=pl.DeviceIdType.MESH,
+        )
+
+    def ring_arrival(direction, step, chunk):
+        piece = held.at[
+            owner_of(direction, step + 1),
+            pl.ds(direction * half + chunk * chunk_rows, chunk_rows),
+        ]
+        return pltpu.make_async_remote_copy(
+            src_ref=piece,
+            dst_ref=piece,
+            send_sem=ring_send.at[direction, step, chunk],
+            recv_sem=ring_recv.at[direction, step, chunk],
+            device_id={"wide": targets[direction]},
+            device_id_type=pl.DeviceIdType.MESH,
+        )
+
+    def with_difference(block):
+        current = block.astype(jnp.float32)
+        places = lax.broadcasted_iota(jnp.int32, current.shape, 0) & (length - 1)
+        previous = jnp.where(places == 0, 0.0, pltpu.roll(current, 1, 0))
+        return current, previous - current
+
+    def add_hidden(direction, step):
+        owner = owner_of(direction, step)
+        rows = pl.ds(direction * half, half)
+        feature_rows = pl.ds(pl.multiple_of(owner * columns, columns), columns)
+        current, difference = with_difference(held[owner, rows])
+        mixed = (current + difference * opening_ref[:, feature_rows]).astype(jnp.bfloat16)
+        term = jnp.dot(mixed, left[feature_rows, :], preferred_element_type=jnp.float32)
+        if step == 0:
+            hidden_sum[rows, :] = term
+        else:
+            hidden_sum[rows, :] += term
+
+    def r_copy(bank, part):
+        return pltpu.make_async_remote_copy(
+            src_ref=r_send.at[bank, part],
+            dst_ref=r_recv.at[w_me],
+            send_sem=r_send_sems.at[bank, part],
+            recv_sem=r_recv_sems.at[w_me],
+            device_id={"wide": n_me * share + part, "narrow": bank},
+            device_id_type=pl.DeviceIdType.MESH,
+        )
+
+    def r_self(bank, part):
+        return pltpu.make_async_copy(r_send.at[bank, part], r_recv.at[w_me], self_sems.at[0])
+
+    def r_arrival(prompt):
+        return pltpu.make_async_remote_copy(
+            src_ref=r_send.at[0, 0],
+            dst_ref=r_recv.at[prompt],
+            send_sem=r_send_sems.at[0, 0],
+            recv_sem=r_recv_sems.at[prompt],
+            device_id={"wide": prompt, "narrow": half_owner},
+            device_id_type=pl.DeviceIdType.MESH,
+        )
+
+    def y_copy(prompt):
+        return pltpu.make_async_remote_copy(
+            src_ref=y_send.at[prompt],
+            dst_ref=y_recv.at[n_me, place_in_half],
+            send_sem=y_send_sems.at[prompt],
+            recv_sem=y_recv_sems.at[n_me, place_in_half],
+            device_id={"wide": prompt, "narrow": half_owner},
+            device_id_type=pl.DeviceIdType.MESH,
+        )
+
+    def y_self(prompt):
+        return pltpu.make_async_copy(
+            y_send.at[prompt], y_recv.at[n_me, place_in_half], self_sems.at[1]
+        )
+
+    def y_arrival(bank, part):
+        return pltpu.make_async_remote_copy(
+            src_ref=y_send.at[0],
+            dst_ref=y_recv.at[bank, part],
+            send_sem=y_send_sems.at[0],
+            recv_sem=y_recv_sems.at[bank, part],
+            device_id={"wide": n_me * share + part, "narrow": bank},
+            device_id_type=pl.DeviceIdType.MESH,
+        )
+
+    def generated_is_mine(bank, part):
+        return jnp.logical_and(n_me * share + part == w_me, n_me == bank)
+
+    def prompt_is_mine(prompt):
+        return jnp.logical_and(w_me == prompt, n_me == half_owner)
+
+    pl.semaphore_wait(barrier, wide * narrow - 1)
+    for chunk in range(chunks):
+        for direction in range(2):
+            ring_copy(direction, 0, chunk).start()
+
+    ones = jnp.where(
+        lax.broadcasted_iota(jnp.int32, (lane_count, lane_count), 0) & -head
+        == lax.broadcasted_iota(jnp.int32, (lane_count, lane_count), 1) & -head,
+        1.0,
+        0.0,
+    ).astype(jnp.bfloat16)
+    first_head = pl.multiple_of(n_me * (generated // head), generated // head)
+    rewards = reward_ref[pl.ds(first_head, generated // head), :]
+    reward_line = jnp.concatenate(
+        [rewards[number : number + 1, :] for number in range(generated // head)], axis=1
+    )
+    pair_rows = {}
+    for bank in range(banks):
+        r_all = r_ref[bank].astype(jnp.float32)
+        k_all = k_ref[bank].astype(jnp.float32)
+        w_all = jnp.exp(-jnp.exp(w_ref[bank].astype(jnp.float32)))
+        for step in range(steps):
+            lagged = r_all[step : step + 1]
+            for earlier in range(step, -1, -1):
+                line = lagged * k_all[earlier : earlier + 1]
+                if earlier == step:
+                    line = line * reward_line
+                row = len(pair_rows)
+                pair_rows[bank, step, earlier] = row
+                pairs[row : row + 1, :] = line
+                if earlier < step:
+                    lagged = lagged * w_all[earlier : earlier + 1]
+            for part in range(share):
+                r_send[bank, part, step : step + 1, :] = lagged[
+                    :, part * columns : (part + 1) * columns
+                ]
+    for bank in range(banks):
+        for part in range(share):
+
+            @pl.when(generated_is_mine(bank, part))
+            def _():
+                r_self(bank, part).start()
+
+            @pl.when(jnp.logical_not(generated_is_mine(bank, part)))
+            def _():
+                r_copy(bank, part).start()
+
+    loads[0].wait()
+    for direction in range(2):
+        add_hidden(direction, 0)
+    for step in range(1, wide - 1):
+        for chunk in range(chunks):
+            for direction in range(2):
+                ring_arrival(direction, step - 1, chunk).wait_recv()
+                ring_copy(direction, step, chunk).start()
+        for direction in range(2):
+            add_hidden(direction, step)
+        if step == 1:
+            sums = segment_sums(pairs[...], ones)
+            for bank in range(banks):
+                v_all = v_ref[bank].astype(jnp.float32)
+                for now in range(steps):
+                    line = None
+                    for earlier in range(now + 1):
+                        row = pair_rows[bank, now, earlier]
+                        term = sums[row : row + 1, :] * v_all[earlier : earlier + 1]
+                        line = term if line is None else line + term
+                    own_part[bank * steps + now : bank * steps + now + 1, :] = line
+    for load in loads[1:]:
+        load.wait()
+    for chunk in range(chunks):
+        for direction in range(2):
+            ring_arrival(direction, wide - 2, chunk).wait_recv()
+    for direction in range(2):
+        add_hidden(direction, wide - 1)
+
+    hidden = jnp.tanh(hidden_sum[...]).astype(jnp.bfloat16)
+    rank = right.shape[1]
+    hidden_parts = [hidden[:, branch * rank : (branch + 1) * rank] for branch in range(3)]
+    transposed = (((1,), (1,)), ((), ()))
+    for block in range(wide):
+        span = slice(block * columns, (block + 1) * columns)
+        current, difference = with_difference(held[block])
+        mixed = []
+        for branch in range(3):
+            shift = jnp.dot(
+                hidden_parts[branch], right[branch, :, span], preferred_element_type=jnp.float32
+            )
+            mixed.append(
+                (current + difference * (blends_ref[branch : branch + 1, span] + shift)).astype(
+                    jnp.bfloat16
+                )
+            )
+        decay_term = jnp.dot(mixed[0], fading_left[span, :], preferred_element_type=jnp.float32)
+        key_term = lax.dot_general(
+            mixed[1], address[:, span], transposed, preferred_element_type=jnp.float32
+        )
+        value_term = lax.dot_general(
+            mixed[2], payload[:, span], transposed, preferred_element_type=jnp.float32
+        )
+        if block == 0:
+            decay_sum[...] = decay_term
+            key_sum[...] = key_term
+            value_sum[...] = value_term
+        else:
+            decay_sum[...] += decay_term
+            key_sum[...] += key_term
+            value_sum[...] += value_term
+
+    decay_hidden = jnp.tanh(decay_sum[...]).astype(jnp.bfloat16)
+    rates = jnp.exp(
+        fixed_ref[...]
+        + jnp.dot(decay_hidden, fading_right_ref[...], preferred_element_type=jnp.float32)
+    )
+    row_ids = lax.broadcasted_iota(jnp.int32, (tokens, tokens), 0)
+    column_ids = lax.broadcasted_iota(jnp.int32, (tokens, tokens), 1)
+    row_limit = jnp.zeros((tokens, 1), jnp.int32)
+    column_limit = jnp.zeros((tokens, tokens), jnp.int32)
+    row_line = lax.broadcasted_iota(jnp.int32, (tokens, 1), 0)
+    for prompt in range(bank_rows):
+        span_now = spans_ref[0, prompt]
+        row_limit = jnp.where(row_line & -length == prompt * length, span_now, row_limit)
+        column_limit = jnp.where(column_ids & -length == prompt * length, span_now, column_limit)
+    later = jnp.where(
+        (row_ids & -length == column_ids & -length)
+        & (column_ids > row_ids)
+        & (column_ids & (length - 1) < column_limit),
+        1.0,
+        0.0,
+    ).astype(jnp.bfloat16)
+    high = rates.astype(jnp.bfloat16)
+    low = (rates - high.astype(jnp.float32)).astype(jnp.bfloat16)
+    remaining = jnp.dot(later, high, preferred_element_type=jnp.float32) + jnp.dot(
+        later, low, preferred_element_type=jnp.float32
+    )
+    weights = jnp.where(row_line & (length - 1) < row_limit, jnp.exp(-remaining), 0.0)
+    weighted = (
+        key_sum[...].astype(jnp.bfloat16).astype(jnp.float32) * weights
+    ).astype(jnp.bfloat16)
+    values = value_sum[...].astype(jnp.bfloat16)
+
+    for prompt in range(bank_rows):
+
+        @pl.when(prompt_is_mine(prompt))
+        def _():
+            for bank in range(banks):
+                for part in range(share):
+
+                    @pl.when(generated_is_mine(bank, part))
+                    def _():
+                        r_self(bank, part).wait()
+
+        @pl.when(jnp.logical_not(prompt_is_mine(prompt)))
+        def _():
+            r_arrival(prompt).wait_recv()
+
+    asked = jnp.concatenate([r_recv[prompt] for prompt in range(bank_rows)], axis=0)
+    asked_rows = bank_rows * steps
+    lane_heads = lax.broadcasted_iota(jnp.int32, (asked_rows, columns), 1) & -head
+    heads = columns // head
+    spread = jnp.concatenate(
+        [jnp.where(lane_heads == number * head, asked, 0.0) for number in range(heads)], axis=0
+    ).astype(jnp.bfloat16)
+    scores = lax.dot_general(spread, weighted, transposed, preferred_element_type=jnp.float32)
+    score_rows = lax.broadcasted_iota(jnp.int32, scores.shape, 0) & (asked_rows - 1)
+    score_columns = lax.broadcasted_iota(jnp.int32, scores.shape, 1)
+    kept = jnp.zeros(scores.shape, jnp.float32)
+    for prompt in range(bank_rows):
+        kept = jnp.where(
+            (score_rows & -steps == prompt * steps)
+            & (score_columns & -length == prompt * length),
+            scores,
+            kept,
+        )
+    answers = jnp.dot(kept.astype(jnp.bfloat16), values, preferred_element_type=jnp.float32)
+    answer = jnp.zeros((asked_rows, columns), jnp.float32)
+    for number in range(heads):
+        answer = jnp.where(
+            lane_heads == number * head,
+            answers[number * asked_rows : (number + 1) * asked_rows],
+            answer,
+        )
+    for prompt in range(bank_rows):
+        y_send[prompt] = answer[prompt * steps : (prompt + 1) * steps]
+    for prompt in range(bank_rows):
+
+        @pl.when(prompt_is_mine(prompt))
+        def _():
+            y_self(prompt).start()
+
+        @pl.when(jnp.logical_not(prompt_is_mine(prompt)))
+        def _():
+            y_copy(prompt).start()
+
+    gate_lines = []
+    for bank in range(banks):
+        gate = g_ref[bank].astype(jnp.float32)
+        gate_lines.append(gate / (1.0 + jnp.exp(-gate)))
+    half_columns = pl.ds(pl.multiple_of(n_me * generated, generated), generated)
+    gain = scaling_ref[:, half_columns]
+    bias = offset_ref[:, half_columns]
+
+    for step in range(wide - 1):
+        for chunk in range(chunks):
+            for direction in range(2):
+                ring_copy(direction, step, chunk).wait_send()
+    for bank in range(banks):
+        for part in range(share):
+
+            @pl.when(jnp.logical_not(generated_is_mine(bank, part)))
+            def _():
+                r_copy(bank, part).wait_send()
+
+    for bank in range(banks):
+        for part in range(share):
+
+            @pl.when(generated_is_mine(bank, part))
+            def _():
+                for prompt in range(bank_rows):
+
+                    @pl.when(prompt_is_mine(prompt))
+                    def _():
+                        y_self(prompt).wait()
+
+            @pl.when(jnp.logical_not(generated_is_mine(bank, part)))
+            def _():
+                y_arrival(bank, part).wait_recv()
+
+    received = jnp.concatenate(
+        [
+            jnp.concatenate([y_recv[bank, part] for part in range(share)], axis=1)
+            for bank in range(banks)
+        ],
+        axis=0,
+    )
+    y = received + own_part[...]
+    centred = y - segment_sums(y, ones) * (1.0 / head)
+    variance = segment_sums(centred * centred, ones) * (1.0 / head)
+    normed = centred * lax.rsqrt(variance + norm_eps) * gain + bias
+    for bank in range(banks):
+        out_ref[bank] = (normed[bank * steps : (bank + 1) * steps] * gate_lines[bank]).astype(
+            out_ref.dtype
+        )
+    for prompt in range(bank_rows):
+
+        @pl.when(jnp.logical_not(prompt_is_mine(prompt)))
+        def _():
+            y_copy(prompt).wait_send()
+
+
+def mixing(wide, narrow, *operands):
+    spans, local = operands[0], operands[1]
+    tokens, columns = local.shape
+    bank_rows = spans.shape[1]
+    features = operands[2].shape[1]
+    left, right, fading_left = operands[4], operands[5], operands[7]
+    address, payload = operands[9], operands[10]
+    banks, steps, generated = operands[14].shape
+    share = wide // narrow
+    chunks = bank_rows // 2
+    pair_count = banks * steps * (steps + 1) // 2
+    vmem = pl.BlockSpec(memory_space=pltpu.VMEM)
+    far = pl.BlockSpec(memory_space=pl.ANY)
+    specs = [vmem] * len(operands)
+    specs[0] = pl.BlockSpec(memory_space=pltpu.SMEM)
+    for number in (4, 5, 7, 9, 10):
+        specs[number] = far
+    f32 = jnp.float32
+    dma = pltpu.SemaphoreType.DMA
+    return pl.pallas_call(
+        functools.partial(mixing_body, wide, narrow),
+        out_shape=jax.ShapeDtypeStruct((banks, steps, generated), jnp.bfloat16),
+        in_specs=specs,
+        out_specs=vmem,
+        scratch_shapes=[
+            pltpu.VMEM((wide, tokens, columns), jnp.bfloat16),
+            pltpu.VMEM(left.shape, left.dtype),
+            pltpu.VMEM(right.shape, right.dtype),
+            pltpu.VMEM(fading_left.shape, fading_left.dtype),
+            pltpu.VMEM(address.shape, address.dtype),
+            pltpu.VMEM(payload.shape, payload.dtype),
+            pltpu.VMEM((tokens, left.shape[1]), f32),
+            pltpu.VMEM((tokens, columns), f32),
+            pltpu.VMEM((tokens, columns), f32),
+            pltpu.VMEM((tokens, fading_left.shape[1]), f32),
+            pltpu.VMEM((pair_count, generated), f32),
+            pltpu.VMEM((banks * steps, generated), f32),
+            pltpu.VMEM((banks, share, steps, columns), f32),
+            pltpu.VMEM((bank_rows, steps, columns), f32),
+            pltpu.VMEM((bank_rows, steps, columns), f32),
+            pltpu.VMEM((banks, share, steps, columns), f32),
+            dma((5,)),
+            dma((2, wide - 1, chunks)),
+            dma((2, wide - 1, chunks)),
+            dma((banks, share)),
+            dma((bank_rows,)),
+            dma((bank_rows,)),
+            dma((banks, share)),
+            dma((2,)),
+        ],
+        compiler_params=pltpu.CompilerParams(
+            collective_id=0, has_side_effects=True, vmem_limit_bytes=40 * 2**20
+        ),
+        name="mix_and_generate",
+    )(*operands)
+
+
+def power_of_two(number):
+    return number > 0 and number & (number - 1) == 0
+
+
+def fits_kernels(wide, narrow, ids, table, reward, acceptance):
+    bank_rows, length = ids.shape[1], ids.shape[2]
+    columns = table.shape[0]
+    banks, prompts, steps, generated = acceptance.shape
+    return (
+        prompts == 1
+        and wide % 2 == 0
+        and wide > 2
+        and wide % narrow == 0
+        and banks == narrow
+        and bank_rows == wide
+        and length % 16 == 0
+        and columns % lane_count == 0
+        and table.shape[1] % lane_count == 0
+        and generated == columns * (wide // narrow)
+        and lane_count % reward.shape[1] == 0
+        and all(power_of_two(size) for size in (length, steps, bank_rows, reward.shape[1]))
+        and columns * length * bank_rows * lane_count * 2 <= 2**25
+    )
+
+
 def per_device(
     context_symbol_ids,
     context_symbol_spans,
@@ -148,6 +763,39 @@
     generated_fading_scores,
     generated_valve_scores,
 ):
+    wide, narrow = lax.axis_size("wide"), lax.axis_size("narrow")
+    if fits_kernels(
+        wide,
+        narrow,
+        context_symbol_ids,
+        symbol_vector_lookup,
+        present_symbol_reward,
+        generated_acceptance,
+    ):
+        result = mixing(
+            wide,
+            narrow,
+            context_symbol_spans,
+            gather_tokens(context_symbol_ids, symbol_vector_lookup),
+            opening_lagged_blend[None],
+            lagged_blend_weights,
+            blending_left_operand,
+            blending_right_operands,
+            fixed_fading_scores[None],
+            fading_left_operand,
+            fading_right_operand,
+            address_projector,
+            payload_projector,
+            present_symbol_reward,
+            cluster_scaling_weight[None],
+            cluster_scaling_offset[None],
+            generated_acceptance[:, 0],
+            generated_addresses[:, 0],
+            generated_payloads[:, 0],
+            generated_fading_scores[:, 0],
+            generated_valve_scores[:, 0],
+        )
+        return result[:, None]
     bank_rows = context_symbol_ids.shape[1]
     length = context_symbol_ids.shape[2]
     columns = symbol_vector_lookup.shape[0]

time: 183 us -> 64 us (0.35)
  waiting for transfers between devices: 63.1 us -> 0 us
  Pallas kernels: 0 us -> 47 us
  local copies, waits for them, and re-layouts: 57.6 us -> 16.1 us
  matrix products: 29.9 us -> 0 us
  between operations: 13.8 us -> 0.11 us
  blocking collectives: 6.56 us -> 0 us
  starting transfers between devices: 5.37 us -> 0 us
  other arithmetic: 4.89 us -> 0 us
    pallas_call x0 -> x2, Pallas kernels: none -> 47 us  [the longest x1 37.9 us: mixing(): pl.pallas_call(functools.partial(mixing_body, wide, narrow), out_shape=ja...]
    all_gather x1 -> x0, waiting for transfers between devices: 39.2 us -> none  [per_device(): gathered = lax.all_gather(picked, 'wide', axis=0, tiled=True).T]
    dot_general x10 -> x0, matrix products: 29.9 us -> none  [the longest x4 13.7 us: generation_iterations(): jnp.einsum('...hi,...hij->...hj', present_acceptance, recurrent_memories,...]
    unnamed x33 -> x38, local copies, waits for them, and re-layouts: 44.4 us -> 16.1 us
    all_to_all x1 -> x0, waiting for transfers between devices: 23.9 us -> none  [per_device(): lax.all_to_all(recurrent_memories.reshape(1, bank_rows, head_local, atten...]
    all_to_all x1 -> x0, blocking collectives: 6.56 us -> none  [per_device(): lax.all_to_all(lax.all_to_all(recurrent_memories.reshape(1, bank_rows, he...]
    another operation x8 -> x0, local copies, waits for them, and re-layouts: 5.6 us -> none  [the longest x1 2.92 us: per_device(): recurrent_memories.reshape(1, bank_rows, head_local, attender_width * att...]
    all_to_all x1 -> x0, starting transfers between devices: 5.37 us -> none  [per_device(): lax.all_to_all(recurrent_memories.reshape(1, bank_rows, head_local, atten...]
  transfers between devices with their start and end apart: 2 -> 0, of which waited for: 2 -> 0; matrix products, arithmetic and copies ran while one was open for 0% -> 0% of each run, Pallas kernels for 0% -> 0%
where the time goes in v1:
time: 64 us; the launch traced here: 63.2 us
  Pallas kernels  47 us (73%)
  local copies, waits for them, and re-layouts  16.1 us (25%)
    pallas_call x1, Pallas kernels, mixing(): pl.pallas_call(functools.partial(mixing_body, wide, narrow), out_shape=ja...  37.9 us
    unnamed x38, local copies, waits for them, and re-layouts  16.1 us
    pallas_call x1, Pallas kernels, gather_tokens(): pl.pallas_call(gather_body, out_shape=jax.ShapeDtypeStruct((rows * length...  9.06 us

profile of v1, /device:TPU:1, one launch (start us, length us, event | category | flops | bytes accessed | tf_op | source)
XLA Modules:
  0.0 63.2 jit_solution(5317644827511590836)
XLA Ops:
  0.0 0.0 copy-start.15
  0.0 0.7 %copy-done.15 = s32[1,8,16]{2,1,0:T(8,128)S(1)} copy-done((s32[1,8,16]{2,1,0:T(8,128)S(1)}, s32[1,8,16]{2,1,0:T(8,128)}, u32[]{:S(2)}) %copy-start.15) | copy-done | bytes 536
  0.7 0.0 copy-start.4
  0.7 0.0 copy-start.5
  0.7 0.0 copy-start.6
  0.7 0.0 copy-start.7
  0.7 0.0 copy-start.12
  0.7 9.1 %pick_tokens.1.local_ref = bf16[128,512]{1,0:T(8,128)(2,1)S(1)} custom-call(s32[1,8,16]{2,1,0:T(8,128)S(1)} %copy-done.15, bf16[512,32768]{1,0:T(8,128)(2,1)} %table_ref.1), custom_call_target="tpu_custom_call" | custom-call | tf_op jit(solution)/shard_map/pick_tokens/pallas_call | solution.py:177
  9.8 0.0 copy-start.3
  9.8 3.2 %copy.21.left_hbm = bf16[4096,192]{1,0:T(8,128)(2,1)S(1)} copy(bf16[4096,192]{0,1:T(8,128)(2,1)} %param.25) | data formatting | bytes 3145728 | tf_op args[5]
  13.0 0.0 copy-done.4
  13.0 0.0 copy-done.5
  13.1 0.0 copy-done.6
  13.1 0.0 copy-done.7
  13.1 0.0 copy-done.12
  13.1 0.0 copy-done.3
  13.1 0.0 copy-start
  13.1 2.2 %copy-done = bf16[512,4096]{1,0:T(8,128)(2,1)S(1)} copy-done((bf16[512,4096]{1,0:T(8,128)(2,1)S(1)}, bf16[512,4096]{1,0:T(8,128)(2,1)}, u32[]{:S(2)}) %copy-start) | copy-done | bytes 4194328
  15.3 0.0 copy-start.1
  15.3 2.2 %copy-done.1 = bf16[512,4096]{1,0:T(8,128)(2,1)S(1)} copy-done((bf16[512,4096]{1,0:T(8,128)(2,1)S(1)}, bf16[512,4096]{1,0:T(8,128)(2,1)}, u32[]{:S(2)}) %copy-start.1) | copy-done | bytes 4194328
  17.5 0.0 copy-start.2
  17.5 1.4 %copy-done.2 = bf16[3,64,4096]{2,1,0:T(8,128)(2,1)S(1)} copy-done((bf16[3,64,4096]{2,1,0:T(8,128)(2,1)S(1)}, bf16[3,64,4096]{2,1,0:T(8,128)(2,1)}, u32[]{:S(2)}) %copy-start.2) | copy-done | bytes 1572888
  18.9 0.8 %copy-done.8 = bf16[2,1,4,2048]{3,2,1,0:T(4,128)(2,1)S(1)} copy-done((bf16[2,1,4,2048]{3,2,1,0:T(4,128)(2,1)S(1)}, bf16[2,1,4,2048]{3,2,1,0:T(4,128)(2,1)}, u32[]{:S(2)}) %copy-start.8) | copy-done | bytes 32792
  19.6 0.8 %copy-done.9 = bf16[2,1,4,2048]{3,2,1,0:T(4,128)(2,1)S(1)} copy-done((bf16[2,1,4,2048]{3,2,1,0:T(4,128)(2,1)S(1)}, bf16[2,1,4,2048]{3,2,1,0:T(4,128)(2,1)}, u32[]{:S(2)}) %copy-start.9) | copy-done | bytes 32792
  20.4 0.8 %copy-done.10 = bf16[2,1,4,2048]{3,2,1,0:T(4,128)(2,1)S(1)} copy-done((bf16[2,1,4,2048]{3,2,1,0:T(4,128)(2,1)S(1)}, bf16[2,1,4,2048]{3,2,1,0:T(4,128)(2,1)}, u32[]{:S(2)}) %copy-start.10) | copy-done | bytes 32792
  21.2 0.8 %copy-done.11 = bf16[2,1,4,2048]{3,2,1,0:T(4,128)(2,1)S(1)} copy-done((bf16[2,1,4,2048]{3,2,1,0:T(4,128)(2,1)S(1)}, bf16[2,1,4,2048]{3,2,1,0:T(4,128)(2,1)}, u32[]{:S(2)}) %copy-start.11) | copy-done | bytes 32792
  21.9 0.7 %copy-done.13 = f32[4096]{0:T(1024)S(1)} copy-done((f32[4096]{0:T(1024)S(1)}, f32[4096]{0:T(1024)}, u32[]{:S(2)}) %copy-start.13) | copy-done | bytes 16408
  22.6 0.7 %copy-done.14 = f32[4096]{0:T(1024)S(1)} copy-done((f32[4096]{0:T(1024)S(1)}, f32[4096]{0:T(1024)}, u32[]{:S(2)}) %copy-start.14) | copy-done | bytes 16408
  23.4 0.7 %copy-done.16 = f32[512]{0:T(512)S(1)} copy-done((f32[512]{0:T(512)S(1)}, f32[512]{0:T(512)}, u32[]{:S(2)}) %copy-start.16) | copy-done | bytes 2072
  24.0 0.7 %copy-done.17 = s32[1,8]{1,0:T(1,128)S(1)} copy-done((s32[1,8]{1,0:T(1,128)S(1)}, s32[1,8]{1,0:T(1,128)}, u32[]{:S(2)}) %copy-start.17) | copy-done | bytes 56
  24.7 37.9 %mix_and_generate.1 = bf16[2,4,2048]{2,1,0:T(4,128)(2,1)S(1)} custom-call(s32[1,8]{1,0:T(1,128)S(1)} %copy-done.17, bf16[128,512]{1,0:T(8,128)(2,1)S(1)} %pick_tokens.1.local_ref, f32[1,4096]{1,0:T(1,128)S(1)} %bitcast.18, f32[3,4096]{1,0:T(4,128)S(1)} %copy-done.5, bf16[4096,192]{1,0:T(8,128)(2,1)S(1)} %copy.21.left_hbm, ...), custom_call_target="tpu_custom_call" | custom-call | tf_op jit(solution)/shard_map/mix_and_generate/pallas_call | solution.py:681
  62.6 0.6 copy.24
  (8 shorter events, 0.0 us)
Async XLA Ops:
  0.0 0.7 %copy-start.15 = (s32[1,8,16]{2,1,0:T(8,128)S(1)}, s32[1,8,16]{2,1,0:T(8,128)}, u32[]{:S(2)}) copy-start(s32[1,8,16]{2,1,0:T(8,128)} %ids_ref.1) | copy-start | bytes 1540
  0.7 12.3 %copy-start.4 = (bf16[128,512]{1,0:T(8,128)(2,1)S(1)}, bf16[128,512]{1,0:T(8,128)(2,1)}, u32[]{:S(2)}) copy-start(bf16[128,512]{1,0:T(8,128)(2,1)} %fading_right_ref.1) | copy-start | bytes 393220
  0.7 12.4 %copy-start.5 = (f32[3,4096]{1,0:T(4,128)S(1)}, f32[3,4096]{1,0:T(4,128)}, u32[]{:S(2)}) copy-start(f32[3,4096]{1,0:T(4,128)} %blends_ref.1) | copy-start | bytes 147460
  0.7 12.4 %copy-start.6 = (f32[64,64]{1,0:T(8,128)S(1)}, f32[64,64]{1,0:T(8,128)}, u32[]{:S(2)}) copy-start(f32[64,64]{1,0:T(8,128)} %reward_ref.1) | copy-start | bytes 49156
  0.7 12.4 %copy-start.7 = (bf16[2,1,4,2048]{3,2,1,0:T(4,128)(2,1)S(1)}, bf16[2,1,4,2048]{3,2,1,0:T(4,128)(2,1)}, u32[]{:S(2)}) copy-start(bf16[2,1,4,2048]{3,2,1,0:T(4,128)(2,1)} %param.35) | copy-start | bytes 98308
  0.7 12.4 %copy-start.12 = (f32[4096]{0:T(1024)S(1)}, f32[4096]{0:T(1024)}, u32[]{:S(2)}) copy-start(f32[4096]{0:T(1024)} %param.23) | copy-start | bytes 49156
  9.8 3.3 %copy-start.3 = (bf16[4096,128]{1,0:T(8,128)(2,1)S(1)}, bf16[4096,128]{1,0:T(8,128)(2,1)}, u32[]{:S(2)}) copy-start(bf16[4096,128]{1,0:T(8,128)(2,1)} %fading_left_hbm.1) | copy-start | bytes 3145732
  13.1 2.2 %copy-start = (bf16[512,4096]{1,0:T(8,128)(2,1)S(1)}, bf16[512,4096]{1,0:T(8,128)(2,1)}, u32[]{:S(2)}) copy-start(bf16[512,4096]{1,0:T(8,128)(2,1)} %address_hbm.1) | copy-start | bytes 12582916
  15.3 2.2 %copy-start.1 = (bf16[512,4096]{1,0:T(8,128)(2,1)S(1)}, bf16[512,4096]{1,0:T(8,128)(2,1)}, u32[]{:S(2)}) copy-start(bf16[512,4096]{1,0:T(8,128)(2,1)} %payload_hbm.1) | copy-start | bytes 12582916
  17.5 1.4 %copy-start.2 = (bf16[3,64,4096]{2,1,0:T(8,128)(2,1)S(1)}, bf16[3,64,4096]{2,1,0:T(8,128)(2,1)}, u32[]{:S(2)}) copy-start(bf16[3,64,4096]{2,1,0:T(8,128)(2,1)} %right_hbm.1) | copy-start | bytes 4718596
  18.9 0.8 %copy-start.8 = (bf16[2,1,4,2048]{3,2,1,0:T(4,128)(2,1)S(1)}, bf16[2,1,4,2048]{3,2,1,0:T(4,128)(2,1)}, u32[]{:S(2)}) copy-start(bf16[2,1,4,2048]{3,2,1,0:T(4,128)(2,1)} %param.36) | copy-start | bytes 98308
  19.6 0.8 %copy-start.9 = (bf16[2,1,4,2048]{3,2,1,0:T(4,128)(2,1)S(1)}, bf16[2,1,4,2048]{3,2,1,0:T(4,128)(2,1)}, u32[]{:S(2)}) copy-start(bf16[2,1,4,2048]{3,2,1,0:T(4,128)(2,1)} %param.37) | copy-start | bytes 98308
  20.4 0.8 %copy-start.10 = (bf16[2,1,4,2048]{3,2,1,0:T(4,128)(2,1)S(1)}, bf16[2,1,4,2048]{3,2,1,0:T(4,128)(2,1)}, u32[]{:S(2)}) copy-start(bf16[2,1,4,2048]{3,2,1,0:T(4,128)(2,1)} %param.38) | copy-start | bytes 98308
  21.2 0.8 %copy-start.11 = (bf16[2,1,4,2048]{3,2,1,0:T(4,128)(2,1)S(1)}, bf16[2,1,4,2048]{3,2,1,0:T(4,128)(2,1)}, u32[]{:S(2)}) copy-start(bf16[2,1,4,2048]{3,2,1,0:T(4,128)(2,1)} %param.39) | copy-start | bytes 98308
  21.9 0.7 %copy-start.13 = (f32[4096]{0:T(1024)S(1)}, f32[4096]{0:T(1024)}, u32[]{:S(2)}) copy-start(f32[4096]{0:T(1024)} %param.33) | copy-start | bytes 49156
  22.6 0.7 %copy-start.14 = (f32[4096]{0:T(1024)S(1)}, f32[4096]{0:T(1024)}, u32[]{:S(2)}) copy-start(f32[4096]{0:T(1024)} %param.34) | copy-start | bytes 49156
  23.4 0.7 %copy-start.16 = (f32[512]{0:T(512)S(1)}, f32[512]{0:T(512)}, u32[]{:S(2)}) copy-start(f32[512]{0:T(512)} %param.27) | copy-start | bytes 6148
  24.0 0.7 %copy-start.17 = (s32[1,8]{1,0:T(1,128)S(1)}, s32[1,8]{1,0:T(1,128)}, u32[]{:S(2)}) copy-start(s32[1,8]{1,0:T(1,128)} %spans_ref.1) | copy-start | bytes 100

commit v2 on v1

--- a/solution.py
+++ b/solution.py
@@ -205,54 +205,49 @@
     return jnp.concatenate(parts, axis=1)
 
 
-def mixing_body(
-    wide,
-    narrow,
-    spans_ref,
-    local_ref,
-    opening_ref,
-    blends_ref,
-    left_hbm,
-    right_hbm,
-    fixed_ref,
-    fading_left_hbm,
-    fading_right_ref,
-    address_hbm,
-    payload_hbm,
-    reward_ref,
-    scaling_ref,
-    offset_ref,
-    r_ref,
-    k_ref,
-    v_ref,
-    w_ref,
-    g_ref,
-    out_ref,
-    held,
-    left,
-    right,
-    fading_left,
-    address,
-    payload,
-    hidden_sum,
-    key_sum,
-    value_sum,
-    decay_sum,
-    pairs,
-    own_part,
-    r_send,
-    r_recv,
-    y_send,
-    y_recv,
-    weight_sems,
-    ring_send,
-    ring_recv,
-    r_send_sems,
-    r_recv_sems,
-    y_send_sems,
-    y_recv_sems,
-    self_sems,
-):
+def mixing_body(wide, narrow, local_ref, *refs):
+    sources, out_ref, loaded = refs[:18], refs[18], refs[19:37]
+    (
+        left,
+        r_ref,
+        w_ref,
+        opening_ref,
+        right,
+        blends_ref,
+        fading_left,
+        address,
+        payload,
+        fixed_ref,
+        fading_right_ref,
+        spans_ref,
+        k_ref,
+        v_ref,
+        g_ref,
+        reward_ref,
+        scaling_ref,
+        offset_ref,
+    ) = loaded
+    (
+        held,
+        hidden_sum,
+        key_sum,
+        value_sum,
+        decay_sum,
+        pairs,
+        own_part,
+        r_send,
+        r_recv,
+        y_send,
+        y_recv,
+        load_sems,
+        ring_send,
+        ring_recv,
+        r_send_sems,
+        r_recv_sems,
+        y_send_sems,
+        y_recv_sems,
+        self_sems,
+    ) = refs[37:]
     w_me = lax.axis_index("wide")
     n_me = lax.axis_index("narrow")
     tokens, columns = local_ref.shape
@@ -260,7 +255,7 @@
     length = tokens // bank_rows
     features = opening_ref.shape[1]
     head = reward_ref.shape[1]
-    banks, steps, generated = r_ref.shape
+    banks, _, steps, generated = r_ref.shape
     share = wide // narrow
     half_owner = lax.div(w_me, share)
     place_in_half = lax.rem(w_me, share)
@@ -276,16 +271,8 @@
         )
 
     loads = [
-        pltpu.make_async_copy(source, target, weight_sems.at[number])
-        for number, (source, target) in enumerate(
-            [
-                (left_hbm, left),
-                (right_hbm, right),
-                (fading_left_hbm, fading_left),
-                (address_hbm, address),
-                (payload_hbm, payload),
-            ]
-        )
+        pltpu.make_async_copy(source, target, load_sems.at[number])
+        for number, (source, target) in enumerate(zip(sources, loaded))
     ]
     for load in loads:
         load.start()
@@ -337,6 +324,8 @@
             device_id_type=pl.DeviceIdType.MESH,
         )
 
+    transposed = (((1,), (1,)), ((), ()))
+
     def with_difference(block):
         current = block.astype(jnp.float32)
         places = lax.broadcasted_iota(jnp.int32, current.shape, 0) & (length - 1)
@@ -349,11 +338,9 @@
         feature_rows = pl.ds(pl.multiple_of(owner * columns, columns), columns)
         current, difference = with_difference(held[owner, rows])
         mixed = (current + difference * opening_ref[:, feature_rows]).astype(jnp.bfloat16)
-        term = jnp.dot(mixed, left[feature_rows, :], preferred_element_type=jnp.float32)
-        if step == 0:
-            hidden_sum[rows, :] = term
-        else:
-            hidden_sum[rows, :] += term
+        hidden_sum[rows, :] += lax.dot_general(
+            mixed, left[:, feature_rows], transposed, preferred_element_type=jnp.float32
+        )
 
     def r_copy(bank, part):
         return pltpu.make_async_remote_copy(
@@ -414,35 +401,21 @@
         for direction in range(2):
             ring_copy(direction, 0, chunk).start()
 
-    ones = jnp.where(
-        lax.broadcasted_iota(jnp.int32, (lane_count, lane_count), 0) & -head
-        == lax.broadcasted_iota(jnp.int32, (lane_count, lane_count), 1) & -head,
-        1.0,
-        0.0,
-    ).astype(jnp.bfloat16)
-    first_head = pl.multiple_of(n_me * (generated // head), generated // head)
-    rewards = reward_ref[pl.ds(first_head, generated // head), :]
-    reward_line = jnp.concatenate(
-        [rewards[number : number + 1, :] for number in range(generated // head)], axis=1
-    )
-    pair_rows = {}
+    hidden_sum[...] = jnp.zeros_like(hidden_sum)
+    for load in loads[:4]:
+        load.wait()
     for bank in range(banks):
-        r_all = r_ref[bank].astype(jnp.float32)
-        k_all = k_ref[bank].astype(jnp.float32)
-        w_all = jnp.exp(-jnp.exp(w_ref[bank].astype(jnp.float32)))
+        r_all = r_ref[bank, 0].astype(jnp.float32)
+        w_all = jnp.exp(-jnp.exp(w_ref[bank, 0].astype(jnp.float32)))
+        faded = None
         for step in range(steps):
-            lagged = r_all[step : step + 1]
-            for earlier in range(step, -1, -1):
-                line = lagged * k_all[earlier : earlier + 1]
-                if earlier == step:
-                    line = line * reward_line
-                row = len(pair_rows)
-                pair_rows[bank, step, earlier] = row
-                pairs[row : row + 1, :] = line
-                if earlier < step:
-                    lagged = lagged * w_all[earlier : earlier + 1]
+            line = r_all[step : step + 1]
+            if step > 0:
+                now = w_all[step - 1 : step]
+                faded = now if faded is None else faded * now
+                line = line * faded
             for part in range(share):
-                r_send[bank, part, step : step + 1, :] = lagged[
+                r_send[bank, part, step : step + 1, :] = line[
                     :, part * columns : (part + 1) * columns
                 ]
     for bank in range(banks):
@@ -456,67 +429,70 @@
             def _():
                 r_copy(bank, part).start()
 
-    loads[0].wait()
     for direction in range(2):
         add_hidden(direction, 0)
-    for step in range(1, wide - 1):
+
+    def ring_step(step, carry):
         for chunk in range(chunks):
             for direction in range(2):
                 ring_arrival(direction, step - 1, chunk).wait_recv()
                 ring_copy(direction, step, chunk).start()
         for direction in range(2):
             add_hidden(direction, step)
-        if step == 1:
-            sums = segment_sums(pairs[...], ones)
-            for bank in range(banks):
-                v_all = v_ref[bank].astype(jnp.float32)
-                for now in range(steps):
-                    line = None
-                    for earlier in range(now + 1):
-                        row = pair_rows[bank, now, earlier]
-                        term = sums[row : row + 1, :] * v_all[earlier : earlier + 1]
-                        line = term if line is None else line + term
-                    own_part[bank * steps + now : bank * steps + now + 1, :] = line
-    for load in loads[1:]:
+        return carry
+
+    lax.fori_loop(1, wide - 1, ring_step, 0)
+    for load in loads[4:]:
         load.wait()
+    decay_sum[...] = jnp.zeros_like(decay_sum)
+    key_sum[...] = jnp.zeros_like(key_sum)
+    value_sum[...] = jnp.zeros_like(value_sum)
     for chunk in range(chunks):
         for direction in range(2):
             ring_arrival(direction, wide - 2, chunk).wait_recv()
     for direction in range(2):
         add_hidden(direction, wide - 1)
 
-    hidden = jnp.tanh(hidden_sum[...]).astype(jnp.bfloat16)
-    rank = right.shape[1]
-    hidden_parts = [hidden[:, branch * rank : (branch + 1) * rank] for branch in range(3)]
-    transposed = (((1,), (1,)), ((), ()))
-    for block in range(wide):
-        span = slice(block * columns, (block + 1) * columns)
+    hidden = jnp.tanh(hidden_sum[...])
+    rank = right.shape[0] // 3
+    hidden_lanes = lax.broadcasted_iota(jnp.int32, hidden.shape, 1)
+    hidden_parts = jnp.concatenate(
+        [
+            jnp.where(
+                (hidden_lanes >= branch * rank) & (hidden_lanes < (branch + 1) * rank), hidden, 0.0
+            )
+            for branch in range(3)
+        ],
+        axis=0,
+    ).astype(jnp.bfloat16)
+
+    def project(block, carry):
+        span = pl.ds(pl.multiple_of(block * columns, columns), columns)
         current, difference = with_difference(held[block])
-        mixed = []
-        for branch in range(3):
-            shift = jnp.dot(
-                hidden_parts[branch], right[branch, :, span], preferred_element_type=jnp.float32
-            )
-            mixed.append(
-                (current + difference * (blends_ref[branch : branch + 1, span] + shift)).astype(
-                    jnp.bfloat16
+        shifts = jnp.dot(hidden_parts, right[:, span], preferred_element_type=jnp.float32)
+        mixed = [
+            (
+                current
+                + difference
+                * (
+                    blends_ref[branch : branch + 1, span]
+                    + shifts[branch * tokens : (branch + 1) * tokens]
                 )
-            )
-        decay_term = jnp.dot(mixed[0], fading_left[span, :], preferred_element_type=jnp.float32)
-        key_term = lax.dot_general(
+            ).astype(jnp.bfloat16)
+            for branch in range(3)
+        ]
+        decay_sum[...] += jnp.dot(
+            mixed[0], fading_left[span, :], preferred_element_type=jnp.float32
+        )
+        key_sum[...] += lax.dot_general(
             mixed[1], address[:, span], transposed, preferred_element_type=jnp.float32
         )
-        value_term = lax.dot_general(
+        value_sum[...] += lax.dot_general(
             mixed[2], payload[:, span], transposed, preferred_element_type=jnp.float32
         )
-        if block == 0:
-            decay_sum[...] = decay_term
-            key_sum[...] = key_term
-            value_sum[...] = value_term
-        else:
-            decay_sum[...] += decay_term
-            key_sum[...] += key_term
-            value_sum[...] += value_term
+        return carry
+
+    lax.fori_loop(0, wide, project, 0, unroll=2)
 
     decay_hidden = jnp.tanh(decay_sum[...]).astype(jnp.bfloat16)
     rates = jnp.exp(
@@ -575,14 +551,12 @@
     scores = lax.dot_general(spread, weighted, transposed, preferred_element_type=jnp.float32)
     score_rows = lax.broadcasted_iota(jnp.int32, scores.shape, 0) & (asked_rows - 1)
     score_columns = lax.broadcasted_iota(jnp.int32, scores.shape, 1)
-    kept = jnp.zeros(scores.shape, jnp.float32)
-    for prompt in range(bank_rows):
-        kept = jnp.where(
-            (score_rows & -steps == prompt * steps)
-            & (score_columns & -length == prompt * length),
-            scores,
-            kept,
-        )
+    kept = jnp.where(
+        lax.shift_right_logical(score_rows, steps.bit_length() - 1)
+        == lax.shift_right_logical(score_columns, length.bit_length() - 1),
+        scores,
+        0.0,
+    )
     answers = jnp.dot(kept.astype(jnp.bfloat16), values, preferred_element_type=jnp.float32)
     answer = jnp.zeros((asked_rows, columns), jnp.float32)
     for number in range(heads):
@@ -603,18 +577,58 @@
         def _():
             y_copy(prompt).start()
 
+    ones = jnp.where(
+        lax.broadcasted_iota(jnp.int32, (lane_count, lane_count), 0) & -head
+        == lax.broadcasted_iota(jnp.int32, (lane_count, lane_count), 1) & -head,
+        1.0,
+        0.0,
+    ).astype(jnp.bfloat16)
+    first_head = pl.multiple_of(n_me * (generated // head), generated // head)
+    rewards = reward_ref[pl.ds(first_head, generated // head), :]
+    reward_line = jnp.concatenate(
+        [rewards[number : number + 1, :] for number in range(generated // head)], axis=1
+    )
+    pair_rows = {}
+    for bank in range(banks):
+        r_all = r_ref[bank, 0].astype(jnp.float32)
+        k_all = k_ref[bank, 0].astype(jnp.float32)
+        w_all = jnp.exp(-jnp.exp(w_ref[bank, 0].astype(jnp.float32)))
+        for step in range(steps):
+            lagged = r_all[step : step + 1]
+            for earlier in range(step, -1, -1):
+                line = lagged * k_all[earlier : earlier + 1]
+                if earlier == step:
+                    line = line * reward_line
+                elif earlier > 0:
+                    lagged = lagged * w_all[earlier : earlier + 1]
+                row = len(pair_rows)
+                pair_rows[bank, step, earlier] = row
+                pairs[row : row + 1, :] = line
+    sums = segment_sums(pairs[...], ones)
+    for bank in range(banks):
+        v_all = v_ref[bank, 0].astype(jnp.float32)
+        for now in range(steps):
+            line = None
+            for earlier in range(now + 1):
+                row = pair_rows[bank, now, earlier]
+                term = sums[row : row + 1, :] * v_all[earlier : earlier + 1]
+                line = term if line is None else line + term
+            own_part[bank * steps + now : bank * steps + now + 1, :] = line
     gate_lines = []
     for bank in range(banks):
-        gate = g_ref[bank].astype(jnp.float32)
+        gate = g_ref[bank, 0].astype(jnp.float32)
         gate_lines.append(gate / (1.0 + jnp.exp(-gate)))
     half_columns = pl.ds(pl.multiple_of(n_me * generated, generated), generated)
     gain = scaling_ref[:, half_columns]
     bias = offset_ref[:, half_columns]
 
-    for step in range(wide - 1):
+    def ring_sent(step, carry):
         for chunk in range(chunks):
             for direction in range(2):
                 ring_copy(direction, step, chunk).wait_send()
+        return carry
+
+    lax.fori_loop(0, wide - 1, ring_sent, 0)
     for bank in range(banks):
         for part in range(share):
 
@@ -649,7 +663,7 @@
     variance = segment_sums(centred * centred, ones) * (1.0 / head)
     normed = centred * lax.rsqrt(variance + norm_eps) * gain + bias
     for bank in range(banks):
-        out_ref[bank] = (normed[bank * steps : (bank + 1) * steps] * gate_lines[bank]).astype(
+        out_ref[bank, 0] = (normed[bank * steps : (bank + 1) * steps] * gate_lines[bank]).astype(
             out_ref.dtype
         )
     for prompt in range(bank_rows):
@@ -659,38 +673,32 @@
             y_copy(prompt).wait_send()
 
 
-def mixing(wide, narrow, *operands):
-    spans, local = operands[0], operands[1]
+def mixing(wide, narrow, local, *operands):
     tokens, columns = local.shape
+    left, receptance, fading_left, spans = operands[0], operands[1], operands[6], operands[11]
     bank_rows = spans.shape[1]
-    features = operands[2].shape[1]
-    left, right, fading_left = operands[4], operands[5], operands[7]
-    address, payload = operands[9], operands[10]
-    banks, steps, generated = operands[14].shape
+    banks, _, steps, generated = receptance.shape
     share = wide // narrow
     chunks = bank_rows // 2
     pair_count = banks * steps * (steps + 1) // 2
     vmem = pl.BlockSpec(memory_space=pltpu.VMEM)
     far = pl.BlockSpec(memory_space=pl.ANY)
-    specs = [vmem] * len(operands)
-    specs[0] = pl.BlockSpec(memory_space=pltpu.SMEM)
-    for number in (4, 5, 7, 9, 10):
-        specs[number] = far
     f32 = jnp.float32
     dma = pltpu.SemaphoreType.DMA
     return pl.pallas_call(
         functools.partial(mixing_body, wide, narrow),
-        out_shape=jax.ShapeDtypeStruct((banks, steps, generated), jnp.bfloat16),
-        in_specs=specs,
+        out_shape=jax.ShapeDtypeStruct(receptance.shape, jnp.bfloat16),
+        in_specs=[vmem] + [far] * len(operands),
         out_specs=vmem,
         scratch_shapes=[
+            pltpu.SMEM(operand.shape, operand.dtype)
+            if operand is spans
+            else pltpu.VMEM(operand.shape, operand.dtype)
+            for operand in operands
+        ]
+        + [
             pltpu.VMEM((wide, tokens, columns), jnp.bfloat16),
-            pltpu.VMEM(left.shape, left.dtype),
-            pltpu.VMEM(right.shape, right.dtype),
-            pltpu.VMEM(fading_left.shape, fading_left.dtype),
-            pltpu.VMEM(address.shape, address.dtype),
-            pltpu.VMEM(payload.shape, payload.dtype),
-            pltpu.VMEM((tokens, left.shape[1]), f32),
+            pltpu.VMEM((tokens, left.shape[0]), f32),
             pltpu.VMEM((tokens, columns), f32),
             pltpu.VMEM((tokens, columns), f32),
             pltpu.VMEM((tokens, fading_left.shape[1]), f32),
@@ -700,7 +708,7 @@
             pltpu.VMEM((bank_rows, steps, columns), f32),
             pltpu.VMEM((bank_rows, steps, columns), f32),
             pltpu.VMEM((banks, share, steps, columns), f32),
-            dma((5,)),
+            dma((len(operands),)),
             dma((2, wide - 1, chunks)),
             dma((2, wide - 1, chunks)),
             dma((banks, share)),
@@ -710,10 +718,10 @@
             dma((2,)),
         ],
         compiler_params=pltpu.CompilerParams(
-            collective_id=0, has_side_effects=True, vmem_limit_bytes=40 * 2**20
+            collective_id=0, has_side_effects=True, vmem_limit_bytes=54 * 2**20
         ),
         name="mix_and_generate",
-    )(*operands)
+    )(local, *operands)
 
 
 def power_of_two(number):
@@ -772,30 +780,29 @@
         present_symbol_reward,
         generated_acceptance,
     ):
-        result = mixing(
+        return mixing(
             wide,
             narrow,
-            context_symbol_spans,
             gather_tokens(context_symbol_ids, symbol_vector_lookup),
+            blending_left_operand.T,
+            generated_acceptance,
+            generated_fading_scores,
             opening_lagged_blend[None],
+            blending_right_operands.reshape(-1, blending_right_operands.shape[2]),
             lagged_blend_weights,
-            blending_left_operand,
-            blending_right_operands,
-            fixed_fading_scores[None],
             fading_left_operand,
-            fading_right_operand,
             address_projector,
             payload_projector,
+            fixed_fading_scores[None],
+            fading_right_operand,
+            context_symbol_spans,
+            generated_addresses,
+            generated_payloads,
+            generated_valve_scores,
             present_symbol_reward,
             cluster_scaling_weight[None],
             cluster_scaling_offset[None],
-            generated_acceptance[:, 0],
-            generated_addresses[:, 0],
-            generated_payloads[:, 0],
-            generated_fading_scores[:, 0],
-            generated_valve_scores[:, 0],
-        )
-        return result[:, None]
+        )
     bank_rows = context_symbol_ids.shape[1]
     length = context_symbol_ids.shape[2]
     columns = symbol_vector_lookup.shape[0]

time: 64 us -> 51.8 us (0.81)
  local copies, waits for them, and re-layouts: 16.1 us -> 2.7 us
  Pallas kernels: 47 us -> 48.9 us
    unnamed x38 -> x5, local copies, waits for them, and re-layouts: 16.1 us -> 2.7 us
    pallas_call x1, Pallas kernels: 37.9 us -> 39.8 us  [mixing(): pl.pallas_call(functools.partial(mixing_body, wide, narrow), out_shape=ja...]
where the time goes in v2:
time: 51.8 us; the launch traced here: 51.6 us
  Pallas kernels  48.9 us (94%)
  local copies, waits for them, and re-layouts  2.7 us (5%)
    pallas_call x1, Pallas kernels, mixing(): pl.pallas_call(functools.partial(mixing_body, wide, narrow), out_shape=ja...  39.8 us
    pallas_call x1, Pallas kernels, gather_tokens(): pl.pallas_call(gather_body, out_shape=jax.ShapeDtypeStruct((rows * length...  9.05 us
    unnamed x5, local copies, waits for them, and re-layouts  2.7 us

profile of v2, /device:TPU:1, one launch (start us, length us, event | category | flops | bytes accessed | tf_op | source)
XLA Modules:
  0.0 51.6 jit_solution(12538942865018301119)
XLA Ops:
  0.0 0.0 copy-start.1
  0.0 0.7 %copy-done.1 = s32[1,8,16]{2,1,0:T(8,128)S(1)} copy-done((s32[1,8,16]{2,1,0:T(8,128)S(1)}, s32[1,8,16]{2,1,0:T(8,128)}, u32[]{:S(2)}) %copy-start.1) | copy-done | bytes 536
  0.7 9.1 %pick_tokens.1.local_ref = bf16[128,512]{1,0:T(8,128)(2,1)S(1)} custom-call(s32[1,8,16]{2,1,0:T(8,128)S(1)} %copy-done.1, bf16[512,32768]{1,0:T(8,128)(2,1)} %table_ref.1), custom_call_target="tpu_custom_call" | custom-call | tf_op jit(solution)/shard_map/pick_tokens/pallas_call | solution.py:177
  9.8 0.0 copy-start
  9.8 0.6 %copy-done = bf16[128,512]{1,0:T(8,128)(2,1)} copy-done((bf16[128,512]{1,0:T(8,128)(2,1)}, bf16[128,512]{1,0:T(8,128)(2,1)S(1)}, u32[]{:S(2)}) %copy-start) | copy-done | bytes 131096
  10.4 39.8 %mix_and_generate.1 = bf16[2,1,4,2048]{3,2,1,0:T(4,128)(2,1)} custom-call(bf16[128,512]{1,0:T(8,128)(2,1)} %copy-done, bf16[192,4096]{1,0:T(8,128)(2,1)} %bitcast.6, bf16[2,1,4,2048]{3,2,1,0:T(4,128)(2,1)} %refs_1_.1, bf16[2,1,4,2048]{3,2,1,0:T(4,128)(2,1)} %refs_2_.1, f32[1,4096]{1,0:T(1,128)} %bitcast.8, bf16[192,4096]{1,0:T(8,128)(2,1)} %bitcast.7, ...), custom_call_target="tpu_custom_call" | custom-call | tf_op jit(solution)/shard_map/mix_and_generate/pallas_call | solution.py:688
  50.2 1.4 %copy.22 = bf16[2,1,4,2048]{3,2,1,0:T(4,128)(2,1)} copy(bf16[2,1,4,2048]{3,2,1,0:T(4,128)(2,1)} %mix_and_generate.1) | data formatting | bytes 65536
Async XLA Ops:
  0.0 0.7 %copy-start.1 = (s32[1,8,16]{2,1,0:T(8,128)S(1)}, s32[1,8,16]{2,1,0:T(8,128)}, u32[]{:S(2)}) copy-start(s32[1,8,16]{2,1,0:T(8,128)} %ids_ref.1) | copy-start | bytes 1540
  9.8 0.6 %copy-start = (bf16[128,512]{1,0:T(8,128)(2,1)}, bf16[128,512]{1,0:T(8,128)(2,1)S(1)}, u32[]{:S(2)}) copy-start(bf16[128,512]{1,0:T(8,128)(2,1)S(1)} %pick_tokens.1.local_ref) | copy-start | bytes 393220

commit v3 on v2

--- a/solution.py
+++ b/solution.py
@@ -131,7 +131,7 @@
     ).astype(jnp.bfloat16)
 
 
-def gather_body(ids_ref, table_ref, out_ref, strips, sems):
+def gather_body(ids_ref, table_ref, out_ref, strips, found, sems):
     rows, length = ids_ref.shape[1], ids_ref.shape[2]
     lanes = strips.shape[2] // length
 
@@ -149,26 +149,31 @@
         return carry
 
     lax.fori_loop(0, rows, start, 0)
-    places = lax.broadcasted_iota(jnp.int32, (length, lanes), 0)
-    columns = lax.broadcasted_iota(jnp.int32, (length, lanes), 1)
+    tokens = rows * length
+    depths = lax.broadcasted_iota(jnp.int32, (lanes, tokens), 0)
+    chosen_tokens = lax.broadcasted_iota(jnp.int32, (lanes, tokens), 1)
+    found[...] = jnp.zeros_like(found)
 
     def pick(row, carry):
-        wanted = jnp.zeros((length, lanes), jnp.int32)
-        for place in range(length):
-            wanted = jnp.where(places == place, lax.rem(ids_ref[0, row, place], lanes), wanted)
-        hit = jnp.where(columns == wanted, 1.0, 0.0)
         chosen = jnp.concatenate(
-            [jnp.where(places == place, hit, 0.0) for place in range(length)], axis=1
-        ).astype(jnp.bfloat16)
+            [
+                jnp.where(
+                    (depths == lax.rem(ids_ref[0, row, place], lanes))
+                    & (chosen_tokens == row * length + place),
+                    1.0,
+                    0.0,
+                ).astype(jnp.bfloat16)
+                for place in range(length)
+            ],
+            axis=0,
+        )
         for place in range(length):
             strip(row, place).wait()
-        found = lax.dot_general(
-            chosen, strips[row], (((1,), (1,)), ((), ())), preferred_element_type=jnp.float32
-        )
-        out_ref[pl.ds(pl.multiple_of(row * length, length), length), :] = found.astype(jnp.bfloat16)
+        found[...] += jnp.dot(strips[row], chosen, preferred_element_type=jnp.float32)
         return carry
 
     lax.fori_loop(0, rows, pick, 0)
+    out_ref[...] = found[...].T.astype(jnp.bfloat16)
 
 
 def gather_tokens(ids, table):
@@ -184,6 +189,7 @@
         out_specs=pl.BlockSpec(memory_space=pltpu.VMEM),
         scratch_shapes=[
             pltpu.VMEM((rows, columns, length * lane_count), jnp.bfloat16),
+            pltpu.VMEM((columns, rows * length), jnp.float32),
             pltpu.SemaphoreType.DMA((rows, length)),
         ],
         compiler_params=pltpu.CompilerParams(vmem_limit_bytes=40 * 2**20),
@@ -205,7 +211,7 @@
     return jnp.concatenate(parts, axis=1)
 
 
-def mixing_body(wide, narrow, local_ref, *refs):
+def mixing_body(wide, narrow, chunks, local_ref, *refs):
     sources, out_ref, loaded = refs[:18], refs[18], refs[19:37]
     (
         left,
@@ -240,8 +246,10 @@
         y_send,
         y_recv,
         load_sems,
-        ring_send,
-        ring_recv,
+        line_send,
+        line_recv,
+        cross_send,
+        cross_recv,
         r_send_sems,
         r_recv_sems,
         y_send_sems,
@@ -274,53 +282,41 @@
         pltpu.make_async_copy(source, target, load_sems.at[number])
         for number, (source, target) in enumerate(zip(sources, loaded))
     ]
-    for load in loads:
+    first_loads = 4
+    for load in loads[:first_loads]:
         load.start()
 
     held[w_me] = local_ref[...]
 
-    def index_at(position):
-        return jnp.where(position < wide // 2, 2 * position, 2 * (wide - 1 - position) + 1)
-
-    position = jnp.where(
-        lax.rem(w_me, 2) == 0, lax.div(w_me, 2), wide - 1 - lax.div(w_me, 2)
-    )
-    targets = (
-        index_at(lax.rem(position + 1, wide)),
-        index_at(lax.rem(position + wide - 1, wide)),
-    )
-    half = tokens // 2
-    chunk_rows = length
-    chunks = half // chunk_rows
-
-    def owner_of(direction, step):
-        back = wide - step if direction == 0 else step
-        return index_at(lax.rem(position + back, wide))
-
-    def ring_copy(direction, step, chunk):
+    line_me, side = lax.div(w_me, 2), lax.rem(w_me, 2)
+    partner = 2 * line_me + 1 - side
+    lines = wide // 2
+    chunk_rows = tokens // chunks
+
+    def owner_of(offset, own_side):
+        return 2 * lax.bitwise_xor(line_me, offset) + (side if own_side else 1 - side)
+
+    def line_copy(offset, chunk, arrival=False):
         piece = held.at[
-            owner_of(direction, step), pl.ds(direction * half + chunk * chunk_rows, chunk_rows)
+            owner_of(offset, True) if arrival else w_me, pl.ds(chunk * chunk_rows, chunk_rows)
         ]
         return pltpu.make_async_remote_copy(
             src_ref=piece,
             dst_ref=piece,
-            send_sem=ring_send.at[direction, step, chunk],
-            recv_sem=ring_recv.at[direction, step, chunk],
-            device_id={"wide": targets[direction]},
+            send_sem=line_send.at[offset - 1, chunk],
+            recv_sem=line_recv.at[offset - 1, chunk],
+            device_id={"wide": owner_of(offset, True)},
             device_id_type=pl.DeviceIdType.MESH,
         )
 
-    def ring_arrival(direction, step, chunk):
-        piece = held.at[
-            owner_of(direction, step + 1),
-            pl.ds(direction * half + chunk * chunk_rows, chunk_rows),
-        ]
+    def cross_copy(offset, chunk, arrival=False):
+        piece = held.at[owner_of(offset, not arrival), pl.ds(chunk * chunk_rows, chunk_rows)]
         return pltpu.make_async_remote_copy(
             src_ref=piece,
             dst_ref=piece,
-            send_sem=ring_send.at[direction, step, chunk],
-            recv_sem=ring_recv.at[direction, step, chunk],
-            device_id={"wide": targets[direction]},
+            send_sem=cross_send.at[offset, chunk],
+            recv_sem=cross_recv.at[offset, chunk],
+            device_id={"wide": partner},
             device_id_type=pl.DeviceIdType.MESH,
         )
 
@@ -332,13 +328,11 @@
         previous = jnp.where(places == 0, 0.0, pltpu.roll(current, 1, 0))
         return current, previous - current
 
-    def add_hidden(direction, step):
-        owner = owner_of(direction, step)
-        rows = pl.ds(direction * half, half)
+    def add_hidden(owner):
         feature_rows = pl.ds(pl.multiple_of(owner * columns, columns), columns)
-        current, difference = with_difference(held[owner, rows])
+        current, difference = with_difference(held[owner])
         mixed = (current + difference * opening_ref[:, feature_rows]).astype(jnp.bfloat16)
-        hidden_sum[rows, :] += lax.dot_general(
+        hidden_sum[...] += lax.dot_general(
             mixed, left[:, feature_rows], transposed, preferred_element_type=jnp.float32
         )
 
@@ -398,12 +392,15 @@
 
     pl.semaphore_wait(barrier, wide * narrow - 1)
     for chunk in range(chunks):
-        for direction in range(2):
-            ring_copy(direction, 0, chunk).start()
+        for offset in range(1, lines):
+            line_copy(offset, chunk).start()
+        cross_copy(0, chunk).start()
 
     hidden_sum[...] = jnp.zeros_like(hidden_sum)
-    for load in loads[:4]:
+    for load in loads[:first_loads]:
         load.wait()
+    for load in loads[first_loads:]:
+        load.start()
     for bank in range(banks):
         r_all = r_ref[bank, 0].astype(jnp.float32)
         w_all = jnp.exp(-jnp.exp(w_ref[bank, 0].astype(jnp.float32)))
@@ -429,29 +426,27 @@
             def _():
                 r_copy(bank, part).start()
 
-    for direction in range(2):
-        add_hidden(direction, 0)
-
-    def ring_step(step, carry):
+    add_hidden(w_me)
+
+    def gather_step(offset, carry):
         for chunk in range(chunks):
-            for direction in range(2):
-                ring_arrival(direction, step - 1, chunk).wait_recv()
-                ring_copy(direction, step, chunk).start()
-        for direction in range(2):
-            add_hidden(direction, step)
+            line_copy(offset, chunk, True).wait_recv()
+            cross_copy(offset, chunk).start()
+        add_hidden(owner_of(offset, True))
+        for chunk in range(chunks):
+            cross_copy(offset - 1, chunk, True).wait_recv()
+        add_hidden(owner_of(offset - 1, False))
         return carry
 
-    lax.fori_loop(1, wide - 1, ring_step, 0)
-    for load in loads[4:]:
+    lax.fori_loop(1, lines, gather_step, 0)
+    for load in loads[first_loads:]:
         load.wait()
     decay_sum[...] = jnp.zeros_like(decay_sum)
     key_sum[...] = jnp.zeros_like(key_sum)
     value_sum[...] = jnp.zeros_like(value_sum)
     for chunk in range(chunks):
-        for direction in range(2):
-            ring_arrival(direction, wide - 2, chunk).wait_recv()
-    for direction in range(2):
-        add_hidden(direction, wide - 1)
+        cross_copy(lines - 1, chunk, True).wait_recv()
+    add_hidden(owner_of(lines - 1, False))
 
     hidden = jnp.tanh(hidden_sum[...])
     rank = right.shape[0] // 3
@@ -622,13 +617,11 @@
     gain = scaling_ref[:, half_columns]
     bias = offset_ref[:, half_columns]
 
-    def ring_sent(step, carry):
-        for chunk in range(chunks):
-            for direction in range(2):
-                ring_copy(direction, step, chunk).wait_send()
-        return carry
-
-    lax.fori_loop(0, wide - 1, ring_sent, 0)
+    for chunk in range(chunks):
+        for offset in range(lines):
+            if offset > 0:
+                line_copy(offset, chunk).wait_send()
+            cross_copy(offset, chunk).wait_send()
     for bank in range(banks):
         for part in range(share):
 
@@ -686,7 +679,7 @@
     f32 = jnp.float32
     dma = pltpu.SemaphoreType.DMA
     return pl.pallas_call(
-        functools.partial(mixing_body, wide, narrow),
+        functools.partial(mixing_body, wide, narrow, chunks),
         out_shape=jax.ShapeDtypeStruct(receptance.shape, jnp.bfloat16),
         in_specs=[vmem] + [far] * len(operands),
         out_specs=vmem,
@@ -709,8 +702,10 @@
             pltpu.VMEM((bank_rows, steps, columns), f32),
             pltpu.VMEM((banks, share, steps, columns), f32),
             dma((len(operands),)),
-            dma((2, wide - 1, chunks)),
-            dma((2, wide - 1, chunks)),
+            dma((wide // 2 - 1, chunks)),
+            dma((wide // 2 - 1, chunks)),
+            dma((wide // 2, chunks)),
+            dma((wide // 2, chunks)),
             dma((banks, share)),
             dma((bank_rows,)),
             dma((bank_rows,)),

time: 51.8 us -> 50.5 us (0.975)
  Pallas kernels: 48.9 us -> 47.6 us
    pallas_call x1, Pallas kernels: 39.8 us -> 37.3 us  [mixing(): pl.pallas_call(functools.partial(mixing_body, wide, narrow, chunks), out_...]
    pallas_call x1, Pallas kernels: 9.05 us -> 10.3 us  [gather_tokens(): pl.pallas_call(gather_body, out_shape=jax.ShapeDtypeStruct((rows * length...]
where the time goes in v3:
time: 50.5 us; the launch traced here: 50.3 us
  Pallas kernels  47.6 us (94%)
  local copies, waits for them, and re-layouts  2.7 us (5%)
    pallas_call x1, Pallas kernels, mixing(): pl.pallas_call(functools.partial(mixing_body, wide, narrow, chunks), out_...  37.3 us
    pallas_call x1, Pallas kernels, gather_tokens(): pl.pallas_call(gather_body, out_shape=jax.ShapeDtypeStruct((rows * length...  10.3 us
    unnamed x5, local copies, waits for them, and re-layouts  2.7 us

profile of v3, /device:TPU:1, one launch (start us, length us, event | category | flops | bytes accessed | tf_op | source)
XLA Modules:
  0.0 50.3 jit_solution(2507219468782673075)
XLA Ops:
  0.0 0.0 copy-start.1
  0.0 0.7 %copy-done.1 = s32[1,8,16]{2,1,0:T(8,128)S(1)} copy-done((s32[1,8,16]{2,1,0:T(8,128)S(1)}, s32[1,8,16]{2,1,0:T(8,128)}, u32[]{:S(2)}) %copy-start.1) | copy-done | bytes 536
  0.7 10.3 %pick_tokens.1.local_ref = bf16[128,512]{1,0:T(8,128)(2,1)S(1)} custom-call(s32[1,8,16]{2,1,0:T(8,128)S(1)} %copy-done.1, bf16[512,32768]{1,0:T(8,128)(2,1)} %table_ref.1), custom_call_target="tpu_custom_call" | custom-call | tf_op jit(solution)/shard_map/pick_tokens/pallas_call | solution.py:182
  11.0 0.0 copy-start
  11.0 0.6 %copy-done = bf16[128,512]{1,0:T(8,128)(2,1)} copy-done((bf16[128,512]{1,0:T(8,128)(2,1)}, bf16[128,512]{1,0:T(8,128)(2,1)S(1)}, u32[]{:S(2)}) %copy-start) | copy-done | bytes 131096
  11.6 37.3 %mix_and_generate.1 = bf16[2,1,4,2048]{3,2,1,0:T(4,128)(2,1)} custom-call(bf16[128,512]{1,0:T(8,128)(2,1)} %copy-done, bf16[192,4096]{1,0:T(8,128)(2,1)} %bitcast.6, bf16[2,1,4,2048]{3,2,1,0:T(4,128)(2,1)} %refs_1_.1, bf16[2,1,4,2048]{3,2,1,0:T(4,128)(2,1)} %refs_2_.1, f32[1,4096]{1,0:T(1,128)} %bitcast.8, bf16[192,4096]{1,0:T(8,128)(2,1)} %bitcast.7, ...), custom_call_target="tpu_custom_call" | custom-call | tf_op jit(solution)/shard_map/mix_and_generate/pallas_call | solution.py:681
  48.9 1.4 %copy.22 = bf16[2,1,4,2048]{3,2,1,0:T(4,128)(2,1)} copy(bf16[2,1,4,2048]{3,2,1,0:T(4,128)(2,1)} %mix_and_generate.1) | data formatting | bytes 65536
Async XLA Ops:
  0.0 0.7 %copy-start.1 = (s32[1,8,16]{2,1,0:T(8,128)S(1)}, s32[1,8,16]{2,1,0:T(8,128)}, u32[]{:S(2)}) copy-start(s32[1,8,16]{2,1,0:T(8,128)} %ids_ref.1) | copy-start | bytes 1540
  11.0 0.6 %copy-start = (bf16[128,512]{1,0:T(8,128)(2,1)}, bf16[128,512]{1,0:T(8,128)(2,1)S(1)}, u32[]{:S(2)}) copy-start(bf16[128,512]{1,0:T(8,128)(2,1)S(1)} %pick_tokens.1.local_ref) | copy-start | bytes 393220

commit v4 on v3

--- a/solution.py
+++ b/solution.py
@@ -131,7 +131,7 @@
     ).astype(jnp.bfloat16)
 
 
-def gather_body(ids_ref, table_ref, out_ref, strips, found, sems):
+def gather_body(ids_ref, table_ref, out_ref, strips, sems):
     rows, length = ids_ref.shape[1], ids_ref.shape[2]
     lanes = strips.shape[2] // length
 
@@ -149,31 +149,26 @@
         return carry
 
     lax.fori_loop(0, rows, start, 0)
-    tokens = rows * length
-    depths = lax.broadcasted_iota(jnp.int32, (lanes, tokens), 0)
-    chosen_tokens = lax.broadcasted_iota(jnp.int32, (lanes, tokens), 1)
-    found[...] = jnp.zeros_like(found)
+    places = lax.broadcasted_iota(jnp.int32, (length, lanes), 0)
+    columns = lax.broadcasted_iota(jnp.int32, (length, lanes), 1)
 
     def pick(row, carry):
+        wanted = jnp.zeros((length, lanes), jnp.int32)
+        for place in range(length):
+            wanted = jnp.where(places == place, lax.rem(ids_ref[0, row, place], lanes), wanted)
+        hit = jnp.where(columns == wanted, 1.0, 0.0)
         chosen = jnp.concatenate(
-            [
-                jnp.where(
-                    (depths == lax.rem(ids_ref[0, row, place], lanes))
-                    & (chosen_tokens == row * length + place),
-                    1.0,
-                    0.0,
-                ).astype(jnp.bfloat16)
-                for place in range(length)
-            ],
-            axis=0,
-        )
+            [jnp.where(places == place, hit, 0.0) for place in range(length)], axis=1
+        ).astype(jnp.bfloat16)
         for place in range(length):
             strip(row, place).wait()
-        found[...] += jnp.dot(strips[row], chosen, preferred_element_type=jnp.float32)
+        found = lax.dot_general(
+            chosen, strips[row], (((1,), (1,)), ((), ())), preferred_element_type=jnp.float32
+        )
+        out_ref[pl.ds(pl.multiple_of(row * length, length), length), :] = found.astype(jnp.bfloat16)
         return carry
 
     lax.fori_loop(0, rows, pick, 0)
-    out_ref[...] = found[...].T.astype(jnp.bfloat16)
 
 
 def gather_tokens(ids, table):
@@ -189,7 +184,6 @@
         out_specs=pl.BlockSpec(memory_space=pltpu.VMEM),
         scratch_shapes=[
             pltpu.VMEM((rows, columns, length * lane_count), jnp.bfloat16),
-            pltpu.VMEM((columns, rows * length), jnp.float32),
             pltpu.SemaphoreType.DMA((rows, length)),
         ],
         compiler_params=pltpu.CompilerParams(vmem_limit_bytes=40 * 2**20),
@@ -198,26 +192,28 @@
 
 
 def segment_sums(rows, ones):
-    width = ones.shape[0]
-    high = rows.astype(jnp.bfloat16)
-    low = (rows - high.astype(jnp.float32)).astype(jnp.bfloat16)
-    parts = []
-    for begin in range(0, rows.shape[1], width):
-        stop = begin + width
-        parts.append(
-            jnp.dot(high[:, begin:stop], ones, preferred_element_type=jnp.float32)
-            + jnp.dot(low[:, begin:stop], ones, preferred_element_type=jnp.float32)
-        )
-    return jnp.concatenate(parts, axis=1)
+    count, width = rows.shape[0], ones.shape[0]
+    pieces = rows.shape[1] // width
+    stacked = jnp.concatenate(
+        [rows[:, piece * width : (piece + 1) * width] for piece in range(pieces)], axis=0
+    )
+    high = stacked.astype(jnp.bfloat16)
+    low = (stacked - high.astype(jnp.float32)).astype(jnp.bfloat16)
+    sums = jnp.dot(high, ones, preferred_element_type=jnp.float32) + jnp.dot(
+        low, ones, preferred_element_type=jnp.float32
+    )
+    return jnp.concatenate(
+        [sums[piece * count : (piece + 1) * count] for piece in range(pieces)], axis=1
+    )
 
 
 def mixing_body(wide, narrow, chunks, local_ref, *refs):
     sources, out_ref, loaded = refs[:18], refs[18], refs[19:37]
     (
         left,
+        opening_ref,
         r_ref,
         w_ref,
-        opening_ref,
         right,
         blends_ref,
         fading_left,
@@ -235,7 +231,10 @@
     ) = loaded
     (
         held,
-        hidden_sum,
+        hidden_parts,
+        partial_send,
+        partial_recv,
+        hidden_all,
         key_sum,
         value_sum,
         decay_sum,
@@ -254,14 +253,16 @@
         r_recv_sems,
         y_send_sems,
         y_recv_sems,
-        self_sems,
+        partial_send_sems,
+        partial_recv_sems,
+        hidden_send_sems,
+        hidden_recv_sems,
     ) = refs[37:]
     w_me = lax.axis_index("wide")
     n_me = lax.axis_index("narrow")
     tokens, columns = local_ref.shape
     bank_rows = spans_ref.shape[1]
     length = tokens // bank_rows
-    features = opening_ref.shape[1]
     head = reward_ref.shape[1]
     banks, _, steps, generated = r_ref.shape
     share = wide // narrow
@@ -278,8 +279,11 @@
             device_id_type=pl.DeviceIdType.MESH,
         )
 
+    own_columns = pl.ds(pl.multiple_of(w_me * columns, columns), columns)
     loads = [
-        pltpu.make_async_copy(source, target, load_sems.at[number])
+        pltpu.make_async_copy(
+            source.at[:, own_columns] if number < 2 else source, target, load_sems.at[number]
+        )
         for number, (source, target) in enumerate(zip(sources, loaded))
     ]
     first_loads = 4
@@ -328,12 +332,38 @@
         previous = jnp.where(places == 0, 0.0, pltpu.roll(current, 1, 0))
         return current, previous - current
 
-    def add_hidden(owner):
-        feature_rows = pl.ds(pl.multiple_of(owner * columns, columns), columns)
-        current, difference = with_difference(held[owner])
-        mixed = (current + difference * opening_ref[:, feature_rows]).astype(jnp.bfloat16)
-        hidden_sum[...] += lax.dot_general(
-            mixed, left[:, feature_rows], transposed, preferred_element_type=jnp.float32
+    def partial_copy(offset):
+        other = lax.bitwise_xor(w_me, offset)
+        return pltpu.make_async_remote_copy(
+            src_ref=partial_send.at[other],
+            dst_ref=partial_recv.at[w_me],
+            send_sem=partial_send_sems.at[offset - 1],
+            recv_sem=partial_recv_sems.at[offset - 1],
+            device_id={"wide": other},
+            device_id_type=pl.DeviceIdType.MESH,
+        )
+
+    def partial_arrival(offset):
+        other = lax.bitwise_xor(w_me, offset)
+        return pltpu.make_async_remote_copy(
+            src_ref=partial_send.at[other],
+            dst_ref=partial_recv.at[other],
+            send_sem=partial_send_sems.at[offset - 1],
+            recv_sem=partial_recv_sems.at[offset - 1],
+            device_id={"wide": other},
+            device_id_type=pl.DeviceIdType.MESH,
+        )
+
+    def hidden_copy(offset, arrival=False):
+        other = lax.bitwise_xor(w_me, offset)
+        piece = hidden_all.at[other if arrival else w_me]
+        return pltpu.make_async_remote_copy(
+            src_ref=piece,
+            dst_ref=piece,
+            send_sem=hidden_send_sems.at[offset - 1],
+            recv_sem=hidden_recv_sems.at[offset - 1],
+            device_id={"wide": other},
+            device_id_type=pl.DeviceIdType.MESH,
         )
 
     def r_copy(bank, part):
@@ -346,9 +376,6 @@
             device_id_type=pl.DeviceIdType.MESH,
         )
 
-    def r_self(bank, part):
-        return pltpu.make_async_copy(r_send.at[bank, part], r_recv.at[w_me], self_sems.at[0])
-
     def r_arrival(prompt):
         return pltpu.make_async_remote_copy(
             src_ref=r_send.at[0, 0],
@@ -369,11 +396,6 @@
             device_id_type=pl.DeviceIdType.MESH,
         )
 
-    def y_self(prompt):
-        return pltpu.make_async_copy(
-            y_send.at[prompt], y_recv.at[n_me, place_in_half], self_sems.at[1]
-        )
-
     def y_arrival(bank, part):
         return pltpu.make_async_remote_copy(
             src_ref=y_send.at[0],
@@ -390,14 +412,24 @@
     def prompt_is_mine(prompt):
         return jnp.logical_and(w_me == prompt, n_me == half_owner)
 
+    loads[0].wait()
+    loads[1].wait()
+    current, difference = with_difference(local_ref[...])
+    own_mixed = (current + difference * opening_ref[...]).astype(jnp.bfloat16)
+    own_share = lax.dot_general(
+        own_mixed, left[...], transposed, preferred_element_type=jnp.float32
+    )
+    for prompt in range(wide):
+        partial_send[prompt] = own_share[prompt * length : (prompt + 1) * length]
     pl.semaphore_wait(barrier, wide * narrow - 1)
-    for chunk in range(chunks):
-        for offset in range(1, lines):
+    for offset in range(1, wide):
+        partial_copy(offset).start()
+    for chunk in range(chunks // 2):
+        for offset in range(lines - 1, 0, -1):
             line_copy(offset, chunk).start()
         cross_copy(0, chunk).start()
 
-    hidden_sum[...] = jnp.zeros_like(hidden_sum)
-    for load in loads[:first_loads]:
+    for load in loads[2:first_loads]:
         load.wait()
     for load in loads[first_loads:]:
         load.start()
@@ -418,40 +450,38 @@
     for bank in range(banks):
         for part in range(share):
 
-            @pl.when(generated_is_mine(bank, part))
-            def _():
-                r_self(bank, part).start()
-
             @pl.when(jnp.logical_not(generated_is_mine(bank, part)))
             def _():
                 r_copy(bank, part).start()
 
-    add_hidden(w_me)
-
-    def gather_step(offset, carry):
-        for chunk in range(chunks):
-            line_copy(offset, chunk, True).wait_recv()
-            cross_copy(offset, chunk).start()
-        add_hidden(owner_of(offset, True))
-        for chunk in range(chunks):
-            cross_copy(offset - 1, chunk, True).wait_recv()
-        add_hidden(owner_of(offset - 1, False))
-        return carry
-
-    lax.fori_loop(1, lines, gather_step, 0)
-    for load in loads[first_loads:]:
-        load.wait()
+    @pl.when(n_me == half_owner)
+    def _():
+        r_recv[w_me] = r_send[n_me, place_in_half]
+
+    total = partial_send[w_me]
+    for offset in range(1, wide):
+        partial_arrival(offset).wait_recv()
+        total = total + partial_recv[lax.bitwise_xor(w_me, offset)]
+    hidden_all[w_me] = jnp.tanh(total).astype(jnp.bfloat16)
+    for offset in range(1, wide):
+        hidden_copy(offset).start()
+    for chunk in range(chunks // 2, chunks):
+        for offset in range(lines - 1, 0, -1):
+            line_copy(offset, chunk).start()
+        cross_copy(0, chunk).start()
     decay_sum[...] = jnp.zeros_like(decay_sum)
     key_sum[...] = jnp.zeros_like(key_sum)
     value_sum[...] = jnp.zeros_like(value_sum)
-    for chunk in range(chunks):
-        cross_copy(lines - 1, chunk, True).wait_recv()
-    add_hidden(owner_of(lines - 1, False))
-
-    hidden = jnp.tanh(hidden_sum[...])
+    for load in loads[first_loads:]:
+        load.wait()
+    for offset in range(1, wide):
+        hidden_copy(offset, True).wait_recv()
+    hidden = jnp.concatenate([hidden_all[prompt] for prompt in range(wide)], axis=0).astype(
+        jnp.float32
+    )
     rank = right.shape[0] // 3
     hidden_lanes = lax.broadcasted_iota(jnp.int32, hidden.shape, 1)
-    hidden_parts = jnp.concatenate(
+    hidden_parts[...] = jnp.concatenate(
         [
             jnp.where(
                 (hidden_lanes >= branch * rank) & (hidden_lanes < (branch + 1) * rank), hidden, 0.0
@@ -461,10 +491,10 @@
         axis=0,
     ).astype(jnp.bfloat16)
 
-    def project(block, carry):
+    def project(block):
         span = pl.ds(pl.multiple_of(block * columns, columns), columns)
         current, difference = with_difference(held[block])
-        shifts = jnp.dot(hidden_parts, right[:, span], preferred_element_type=jnp.float32)
+        shifts = jnp.dot(hidden_parts[...], right[:, span], preferred_element_type=jnp.float32)
         mixed = [
             (
                 current
@@ -485,9 +515,22 @@
         value_sum[...] += lax.dot_general(
             mixed[2], payload[:, span], transposed, preferred_element_type=jnp.float32
         )
+
+    def gather_step(offset, carry):
+        for chunk in range(chunks):
+            line_copy(offset, chunk, True).wait_recv()
+            cross_copy(offset, chunk).start()
+        project(owner_of(offset - 1, True))
+        for chunk in range(chunks):
+            cross_copy(offset - 1, chunk, True).wait_recv()
+        project(owner_of(offset - 1, False))
         return carry
 
-    lax.fori_loop(0, wide, project, 0, unroll=2)
+    lax.fori_loop(1, lines, gather_step, 0)
+    project(owner_of(lines - 1, True))
+    for chunk in range(chunks):
+        cross_copy(lines - 1, chunk, True).wait_recv()
+    project(owner_of(lines - 1, False))
 
     decay_hidden = jnp.tanh(decay_sum[...]).astype(jnp.bfloat16)
     rates = jnp.exp(
@@ -523,15 +566,6 @@
 
     for prompt in range(bank_rows):
 
-        @pl.when(prompt_is_mine(prompt))
-        def _():
-            for bank in range(banks):
-                for part in range(share):
-
-                    @pl.when(generated_is_mine(bank, part))
-                    def _():
-                        r_self(bank, part).wait()
-
         @pl.when(jnp.logical_not(prompt_is_mine(prompt)))
         def _():
             r_arrival(prompt).wait_recv()
@@ -564,13 +598,13 @@
         y_send[prompt] = answer[prompt * steps : (prompt + 1) * steps]
     for prompt in range(bank_rows):
 
-        @pl.when(prompt_is_mine(prompt))
-        def _():
-            y_self(prompt).start()
-
         @pl.when(jnp.logical_not(prompt_is_mine(prompt)))
         def _():
             y_copy(prompt).start()
+
+    @pl.when(n_me == half_owner)
+    def _():
+        y_recv[n_me, place_in_half] = y_send[w_me]
 
     ones = jnp.where(
         lax.broadcasted_iota(jnp.int32, (lane_count, lane_count), 0) & -head
@@ -599,6 +633,8 @@
                 row = len(pair_rows)
                 pair_rows[bank, step, earlier] = row
                 pairs[row : row + 1, :] = line
+    for row in range(len(pair_rows), pairs.shape[0]):
+        pairs[row : row + 1, :] = jnp.zeros((1, generated), jnp.float32)
     sums = segment_sums(pairs[...], ones)
     for bank in range(banks):
         v_all = v_ref[bank, 0].astype(jnp.float32)
@@ -622,6 +658,9 @@
             if offset > 0:
                 line_copy(offset, chunk).wait_send()
             cross_copy(offset, chunk).wait_send()
+    for offset in range(1, wide):
+        partial_copy(offset).wait_send()
+        hidden_copy(offset).wait_send()
     for bank in range(banks):
         for part in range(share):
 
@@ -631,14 +670,6 @@
 
     for bank in range(banks):
         for part in range(share):
-
-            @pl.when(generated_is_mine(bank, part))
-            def _():
-                for prompt in range(bank_rows):
-
-                    @pl.when(prompt_is_mine(prompt))
-                    def _():
-                        y_self(prompt).wait()
 
             @pl.when(jnp.logical_not(generated_is_mine(bank, part)))
             def _():
@@ -668,12 +699,12 @@
 
 def mixing(wide, narrow, local, *operands):
     tokens, columns = local.shape
-    left, receptance, fading_left, spans = operands[0], operands[1], operands[6], operands[11]
+    left, receptance, fading_left, spans = operands[0], operands[2], operands[6], operands[11]
     bank_rows = spans.shape[1]
     banks, _, steps, generated = receptance.shape
     share = wide // narrow
     chunks = bank_rows // 2
-    pair_count = banks * steps * (steps + 1) // 2
+    pair_count = -(-(banks * steps * (steps + 1) // 2) // 8) * 8
     vmem = pl.BlockSpec(memory_space=pltpu.VMEM)
     far = pl.BlockSpec(memory_space=pl.ANY)
     f32 = jnp.float32
@@ -686,12 +717,17 @@
         scratch_shapes=[
             pltpu.SMEM(operand.shape, operand.dtype)
             if operand is spans
-            else pltpu.VMEM(operand.shape, operand.dtype)
-            for operand in operands
+            else pltpu.VMEM(
+                (operand.shape[0], columns) if number < 2 else operand.shape, operand.dtype
+            )
+            for number, operand in enumerate(operands)
         ]
         + [
             pltpu.VMEM((wide, tokens, columns), jnp.bfloat16),
-            pltpu.VMEM((tokens, left.shape[0]), f32),
+            pltpu.VMEM((3 * tokens, left.shape[0]), jnp.bfloat16),
+            pltpu.VMEM((wide, tokens // wide, left.shape[0]), f32),
+            pltpu.VMEM((wide, tokens // wide, left.shape[0]), f32),
+            pltpu.VMEM((wide, tokens // wide, left.shape[0]), jnp.bfloat16),
             pltpu.VMEM((tokens, columns), f32),
             pltpu.VMEM((tokens, columns), f32),
             pltpu.VMEM((tokens, fading_left.shape[1]), f32),
@@ -710,7 +746,10 @@
             dma((bank_rows,)),
             dma((bank_rows,)),
             dma((banks, share)),
-            dma((2,)),
+            dma((wide - 1,)),
+            dma((wide - 1,)),
+            dma((wide - 1,)),
+            dma((wide - 1,)),
         ],
         compiler_params=pltpu.CompilerParams(
             collective_id=0, has_side_effects=True, vmem_limit_bytes=54 * 2**20
@@ -780,9 +819,9 @@
             narrow,
             gather_tokens(context_symbol_ids, symbol_vector_lookup),
             blending_left_operand.T,
+            opening_lagged_blend[None],
             generated_acceptance,
             generated_fading_scores,
-            opening_lagged_blend[None],
             blending_right_operands.reshape(-1, blending_right_operands.shape[2]),
             lagged_blend_weights,
             fading_left_operand,

time: 50.5 us -> 52 us (1.030)
  Pallas kernels: 47.6 us -> 49 us
    pallas_call x1, Pallas kernels: 37.3 us -> 40 us  [mixing(): pl.pallas_call(functools.partial(mixing_body, wide, narrow, chunks), out_...]
    pallas_call x1, Pallas kernels: 10.3 us -> 9.05 us  [gather_tokens(): pl.pallas_call(gather_body, out_shape=jax.ShapeDtypeStruct((rows * length...]
where the time goes in v4:
time: 52 us; the launch traced here: 51.7 us
  Pallas kernels  49 us (94%)
  local copies, waits for them, and re-layouts  2.7 us (5%)
    pallas_call x1, Pallas kernels, mixing(): pl.pallas_call(functools.partial(mixing_body, wide, narrow, chunks), out_...  40 us
    pallas_call x1, Pallas kernels, gather_tokens(): pl.pallas_call(gather_body, out_shape=jax.ShapeDtypeStruct((rows * length...  9.05 us
    unnamed x5, local copies, waits for them, and re-layouts  2.7 us

profile of v4, /device:TPU:1, one launch (start us, length us, event | category | flops | bytes accessed | tf_op | source)
XLA Modules:
  0.0 51.7 jit_solution(12198719494633069457)
XLA Ops:
  0.0 0.0 copy-start.1
  0.0 0.7 %copy-done.1 = s32[1,8,16]{2,1,0:T(8,128)S(1)} copy-done((s32[1,8,16]{2,1,0:T(8,128)S(1)}, s32[1,8,16]{2,1,0:T(8,128)}, u32[]{:S(2)}) %copy-start.1) | copy-done | bytes 536
  0.7 9.1 %pick_tokens.1.local_ref = bf16[128,512]{1,0:T(8,128)(2,1)S(1)} custom-call(s32[1,8,16]{2,1,0:T(8,128)S(1)} %copy-done.1, bf16[512,32768]{1,0:T(8,128)(2,1)} %table_ref.1), custom_call_target="tpu_custom_call" | custom-call | tf_op jit(solution)/shard_map/pick_tokens/pallas_call | solution.py:177
  9.8 0.0 copy-start
  9.8 0.6 %copy-done = bf16[128,512]{1,0:T(8,128)(2,1)} copy-done((bf16[128,512]{1,0:T(8,128)(2,1)}, bf16[128,512]{1,0:T(8,128)(2,1)S(1)}, u32[]{:S(2)}) %copy-start) | copy-done | bytes 131096
  10.4 40.0 %mix_and_generate.1 = bf16[2,1,4,2048]{3,2,1,0:T(4,128)(2,1)} custom-call(bf16[128,512]{1,0:T(8,128)(2,1)} %copy-done, bf16[192,4096]{1,0:T(8,128)(2,1)} %bitcast.6, f32[1,4096]{1,0:T(1,128)} %bitcast.8, bf16[2,1,4,2048]{3,2,1,0:T(4,128)(2,1)} %refs_2_.1, bf16[2,1,4,2048]{3,2,1,0:T(4,128)(2,1)} %refs_3_.1, bf16[192,4096]{1,0:T(8,128)(2,1)} %bitcast.7, ...), custom_call_target="tpu_custom_call" | custom-call | tf_op jit(solution)/shard_map/mix_and_generate/pallas_call | solution.py:712
  50.4 1.4 %copy.22 = bf16[2,1,4,2048]{3,2,1,0:T(4,128)(2,1)} copy(bf16[2,1,4,2048]{3,2,1,0:T(4,128)(2,1)} %mix_and_generate.1) | data formatting | bytes 65536
Async XLA Ops:
  0.0 0.7 %copy-start.1 = (s32[1,8,16]{2,1,0:T(8,128)S(1)}, s32[1,8,16]{2,1,0:T(8,128)}, u32[]{:S(2)}) copy-start(s32[1,8,16]{2,1,0:T(8,128)} %ids_ref.1) | copy-start | bytes 1540
  9.8 0.6 %copy-start = (bf16[128,512]{1,0:T(8,128)(2,1)}, bf16[128,512]{1,0:T(8,128)(2,1)S(1)}, u32[]{:S(2)}) copy-start(bf16[128,512]{1,0:T(8,128)(2,1)S(1)} %pick_tokens.1.local_ref) | copy-start | bytes 393220

commit v5 on v3

--- a/solution.py
+++ b/solution.py
@@ -131,7 +131,7 @@
     ).astype(jnp.bfloat16)
 
 
-def gather_body(ids_ref, table_ref, out_ref, strips, found, sems):
+def gather_body(ids_ref, table_ref, out_ref, strips, sems):
     rows, length = ids_ref.shape[1], ids_ref.shape[2]
     lanes = strips.shape[2] // length
 
@@ -149,31 +149,26 @@
         return carry
 
     lax.fori_loop(0, rows, start, 0)
-    tokens = rows * length
-    depths = lax.broadcasted_iota(jnp.int32, (lanes, tokens), 0)
-    chosen_tokens = lax.broadcasted_iota(jnp.int32, (lanes, tokens), 1)
-    found[...] = jnp.zeros_like(found)
+    places = lax.broadcasted_iota(jnp.int32, (length, lanes), 0)
+    columns = lax.broadcasted_iota(jnp.int32, (length, lanes), 1)
 
     def pick(row, carry):
+        wanted = jnp.zeros((length, lanes), jnp.int32)
+        for place in range(length):
+            wanted = jnp.where(places == place, lax.rem(ids_ref[0, row, place], lanes), wanted)
+        hit = jnp.where(columns == wanted, 1.0, 0.0)
         chosen = jnp.concatenate(
-            [
-                jnp.where(
-                    (depths == lax.rem(ids_ref[0, row, place], lanes))
-                    & (chosen_tokens == row * length + place),
-                    1.0,
-                    0.0,
-                ).astype(jnp.bfloat16)
-                for place in range(length)
-            ],
-            axis=0,
-        )
+            [jnp.where(places == place, hit, 0.0) for place in range(length)], axis=1
+        ).astype(jnp.bfloat16)
         for place in range(length):
             strip(row, place).wait()
-        found[...] += jnp.dot(strips[row], chosen, preferred_element_type=jnp.float32)
+        found = lax.dot_general(
+            chosen, strips[row], (((1,), (1,)), ((), ())), preferred_element_type=jnp.float32
+        )
+        out_ref[pl.ds(pl.multiple_of(row * length, length), length), :] = found.astype(jnp.bfloat16)
         return carry
 
     lax.fori_loop(0, rows, pick, 0)
-    out_ref[...] = found[...].T.astype(jnp.bfloat16)
 
 
 def gather_tokens(ids, table):
@@ -189,7 +184,6 @@
         out_specs=pl.BlockSpec(memory_space=pltpu.VMEM),
         scratch_shapes=[
             pltpu.VMEM((rows, columns, length * lane_count), jnp.bfloat16),
-            pltpu.VMEM((columns, rows * length), jnp.float32),
             pltpu.SemaphoreType.DMA((rows, length)),
         ],
         compiler_params=pltpu.CompilerParams(vmem_limit_bytes=40 * 2**20),
@@ -198,26 +192,28 @@
 
 
 def segment_sums(rows, ones):
-    width = ones.shape[0]
-    high = rows.astype(jnp.bfloat16)
-    low = (rows - high.astype(jnp.float32)).astype(jnp.bfloat16)
-    parts = []
-    for begin in range(0, rows.shape[1], width):
-        stop = begin + width
-        parts.append(
-            jnp.dot(high[:, begin:stop], ones, preferred_element_type=jnp.float32)
-            + jnp.dot(low[:, begin:stop], ones, preferred_element_type=jnp.float32)
-        )
-    return jnp.concatenate(parts, axis=1)
+    count, width = rows.shape[0], ones.shape[0]
+    pieces = rows.shape[1] // width
+    stacked = jnp.concatenate(
+        [rows[:, piece * width : (piece + 1) * width] for piece in range(pieces)], axis=0
+    )
+    high = stacked.astype(jnp.bfloat16)
+    low = (stacked - high.astype(jnp.float32)).astype(jnp.bfloat16)
+    sums = jnp.dot(high, ones, preferred_element_type=jnp.float32) + jnp.dot(
+        low, ones, preferred_element_type=jnp.float32
+    )
+    return jnp.concatenate(
+        [sums[piece * count : (piece + 1) * count] for piece in range(pieces)], axis=1
+    )
 
 
 def mixing_body(wide, narrow, chunks, local_ref, *refs):
     sources, out_ref, loaded = refs[:18], refs[18], refs[19:37]
     (
         left,
+        opening_ref,
         r_ref,
         w_ref,
-        opening_ref,
         right,
         blends_ref,
         fading_left,
@@ -235,6 +231,7 @@
     ) = loaded
     (
         held,
+        hidden_parts,
         hidden_sum,
         key_sum,
         value_sum,
@@ -254,14 +251,12 @@
         r_recv_sems,
         y_send_sems,
         y_recv_sems,
-        self_sems,
     ) = refs[37:]
     w_me = lax.axis_index("wide")
     n_me = lax.axis_index("narrow")
     tokens, columns = local_ref.shape
     bank_rows = spans_ref.shape[1]
     length = tokens // bank_rows
-    features = opening_ref.shape[1]
     head = reward_ref.shape[1]
     banks, _, steps, generated = r_ref.shape
     share = wide // narrow
@@ -346,9 +341,6 @@
             device_id_type=pl.DeviceIdType.MESH,
         )
 
-    def r_self(bank, part):
-        return pltpu.make_async_copy(r_send.at[bank, part], r_recv.at[w_me], self_sems.at[0])
-
     def r_arrival(prompt):
         return pltpu.make_async_remote_copy(
             src_ref=r_send.at[0, 0],
@@ -369,11 +361,6 @@
             device_id_type=pl.DeviceIdType.MESH,
         )
 
-    def y_self(prompt):
-        return pltpu.make_async_copy(
-            y_send.at[prompt], y_recv.at[n_me, place_in_half], self_sems.at[1]
-        )
-
     def y_arrival(bank, part):
         return pltpu.make_async_remote_copy(
             src_ref=y_send.at[0],
@@ -392,15 +379,16 @@
 
     pl.semaphore_wait(barrier, wide * narrow - 1)
     for chunk in range(chunks):
+        cross_copy(0, chunk).start()
         for offset in range(1, lines):
             line_copy(offset, chunk).start()
-        cross_copy(0, chunk).start()
-
+
+    for load in loads[2:first_loads]:
+        load.wait()
     hidden_sum[...] = jnp.zeros_like(hidden_sum)
-    for load in loads[:first_loads]:
-        load.wait()
-    for load in loads[first_loads:]:
-        load.start()
+    decay_sum[...] = jnp.zeros_like(decay_sum)
+    key_sum[...] = jnp.zeros_like(key_sum)
+    value_sum[...] = jnp.zeros_like(value_sum)
     for bank in range(banks):
         r_all = r_ref[bank, 0].astype(jnp.float32)
         w_all = jnp.exp(-jnp.exp(w_ref[bank, 0].astype(jnp.float32)))
@@ -418,14 +406,18 @@
     for bank in range(banks):
         for part in range(share):
 
-            @pl.when(generated_is_mine(bank, part))
-            def _():
-                r_self(bank, part).start()
-
             @pl.when(jnp.logical_not(generated_is_mine(bank, part)))
             def _():
                 r_copy(bank, part).start()
 
+    @pl.when(n_me == half_owner)
+    def _():
+        r_recv[w_me] = r_send[n_me, place_in_half]
+
+    for load in loads[first_loads:]:
+        load.start()
+    for load in loads[:2]:
+        load.wait()
     add_hidden(w_me)
 
     def gather_step(offset, carry):
@@ -441,9 +433,6 @@
     lax.fori_loop(1, lines, gather_step, 0)
     for load in loads[first_loads:]:
         load.wait()
-    decay_sum[...] = jnp.zeros_like(decay_sum)
-    key_sum[...] = jnp.zeros_like(key_sum)
-    value_sum[...] = jnp.zeros_like(value_sum)
     for chunk in range(chunks):
         cross_copy(lines - 1, chunk, True).wait_recv()
     add_hidden(owner_of(lines - 1, False))
@@ -451,7 +440,7 @@
     hidden = jnp.tanh(hidden_sum[...])
     rank = right.shape[0] // 3
     hidden_lanes = lax.broadcasted_iota(jnp.int32, hidden.shape, 1)
-    hidden_parts = jnp.concatenate(
+    hidden_parts[...] = jnp.concatenate(
         [
             jnp.where(
                 (hidden_lanes >= branch * rank) & (hidden_lanes < (branch + 1) * rank), hidden, 0.0
@@ -461,33 +450,35 @@
         axis=0,
     ).astype(jnp.bfloat16)
 
-    def project(block, carry):
-        span = pl.ds(pl.multiple_of(block * columns, columns), columns)
-        current, difference = with_difference(held[block])
-        shifts = jnp.dot(hidden_parts, right[:, span], preferred_element_type=jnp.float32)
-        mixed = [
-            (
-                current
-                + difference
-                * (
-                    blends_ref[branch : branch + 1, span]
+    def project(pair, carry):
+        span = pl.ds(pl.multiple_of(pair * 2 * columns, 2 * columns), 2 * columns)
+        mixed = [[], [], []]
+        for member in range(2):
+            block = pair * 2 + member
+            part = pl.ds(pl.multiple_of(block * columns, columns), columns)
+            current, difference = with_difference(held[block])
+            shifts = jnp.dot(
+                hidden_parts[...], right[:, part], preferred_element_type=jnp.float32
+            )
+            for branch in range(3):
+                blend = (
+                    blends_ref[branch : branch + 1, part]
                     + shifts[branch * tokens : (branch + 1) * tokens]
                 )
-            ).astype(jnp.bfloat16)
-            for branch in range(3)
-        ]
+                mixed[branch].append((current + difference * blend).astype(jnp.bfloat16))
+        decayed, keyed, valued = (jnp.concatenate(parts, axis=1) for parts in mixed)
         decay_sum[...] += jnp.dot(
-            mixed[0], fading_left[span, :], preferred_element_type=jnp.float32
+            decayed, fading_left[span, :], preferred_element_type=jnp.float32
         )
         key_sum[...] += lax.dot_general(
-            mixed[1], address[:, span], transposed, preferred_element_type=jnp.float32
+            keyed, address[:, span], transposed, preferred_element_type=jnp.float32
         )
         value_sum[...] += lax.dot_general(
-            mixed[2], payload[:, span], transposed, preferred_element_type=jnp.float32
+            valued, payload[:, span], transposed, preferred_element_type=jnp.float32
         )
         return carry
 
-    lax.fori_loop(0, wide, project, 0, unroll=2)
+    lax.fori_loop(0, lines, project, 0)
 
     decay_hidden = jnp.tanh(decay_sum[...]).astype(jnp.bfloat16)
     rates = jnp.exp(
@@ -523,15 +514,6 @@
 
     for prompt in range(bank_rows):
 
-        @pl.when(prompt_is_mine(prompt))
-        def _():
-            for bank in range(banks):
-                for part in range(share):
-
-                    @pl.when(generated_is_mine(bank, part))
-                    def _():
-                        r_self(bank, part).wait()
-
         @pl.when(jnp.logical_not(prompt_is_mine(prompt)))
         def _():
             r_arrival(prompt).wait_recv()
@@ -564,13 +546,13 @@
         y_send[prompt] = answer[prompt * steps : (prompt + 1) * steps]
     for prompt in range(bank_rows):
 
-        @pl.when(prompt_is_mine(prompt))
-        def _():
-            y_self(prompt).start()
-
         @pl.when(jnp.logical_not(prompt_is_mine(prompt)))
         def _():
             y_copy(prompt).start()
+
+    @pl.when(n_me == half_owner)
+    def _():
+        y_recv[n_me, place_in_half] = y_send[w_me]
 
     ones = jnp.where(
         lax.broadcasted_iota(jnp.int32, (lane_count, lane_count), 0) & -head
@@ -599,6 +581,8 @@
                 row = len(pair_rows)
                 pair_rows[bank, step, earlier] = row
                 pairs[row : row + 1, :] = line
+    for row in range(len(pair_rows), pairs.shape[0]):
+        pairs[row : row + 1, :] = jnp.zeros((1, generated), jnp.float32)
     sums = segment_sums(pairs[...], ones)
     for bank in range(banks):
         v_all = v_ref[bank, 0].astype(jnp.float32)
@@ -632,14 +616,6 @@
     for bank in range(banks):
         for part in range(share):
 
-            @pl.when(generated_is_mine(bank, part))
-            def _():
-                for prompt in range(bank_rows):
-
-                    @pl.when(prompt_is_mine(prompt))
-                    def _():
-                        y_self(prompt).wait()
-
             @pl.when(jnp.logical_not(generated_is_mine(bank, part)))
             def _():
                 y_arrival(bank, part).wait_recv()
@@ -668,12 +644,12 @@
 
 def mixing(wide, narrow, local, *operands):
     tokens, columns = local.shape
-    left, receptance, fading_left, spans = operands[0], operands[1], operands[6], operands[11]
+    left, receptance, fading_left, spans = operands[0], operands[2], operands[6], operands[11]
     bank_rows = spans.shape[1]
     banks, _, steps, generated = receptance.shape
     share = wide // narrow
     chunks = bank_rows // 2
-    pair_count = banks * steps * (steps + 1) // 2
+    pair_count = -(-(banks * steps * (steps + 1) // 2) // 8) * 8
     vmem = pl.BlockSpec(memory_space=pltpu.VMEM)
     far = pl.BlockSpec(memory_space=pl.ANY)
     f32 = jnp.float32
@@ -691,6 +667,7 @@
         ]
         + [
             pltpu.VMEM((wide, tokens, columns), jnp.bfloat16),
+            pltpu.VMEM((3 * tokens, left.shape[0]), jnp.bfloat16),
             pltpu.VMEM((tokens, left.shape[0]), f32),
             pltpu.VMEM((tokens, columns), f32),
             pltpu.VMEM((tokens, columns), f32),
@@ -710,7 +687,6 @@
             dma((bank_rows,)),
             dma((bank_rows,)),
             dma((banks, share)),
-            dma((2,)),
         ],
         compiler_params=pltpu.CompilerParams(
             collective_id=0, has_side_effects=True, vmem_limit_bytes=54 * 2**20
@@ -780,9 +756,9 @@
             narrow,
             gather_tokens(context_symbol_ids, symbol_vector_lookup),
             blending_left_operand.T,
+            opening_lagged_blend[None],
             generated_acceptance,
             generated_fading_scores,
-            opening_lagged_blend[None],
             blending_right_operands.reshape(-1, blending_right_operands.shape[2]),
             lagged_blend_weights,
             fading_left_operand,

time: 50.5 us -> 48.4 us (0.958)
  Pallas kernels: 47.6 us -> 45.4 us
    pallas_call x1, Pallas kernels: 10.3 us -> 9.05 us  [gather_tokens(): pl.pallas_call(gather_body, out_shape=jax.ShapeDtypeStruct((rows * length...]
    pallas_call x1, Pallas kernels: 37.3 us -> 36.4 us  [mixing(): pl.pallas_call(functools.partial(mixing_body, wide, narrow, chunks), out_...]
where the time goes in v5:
time: 48.4 us; the launch traced here: 48.1 us
  Pallas kernels  45.4 us (94%)
  local copies, waits for them, and re-layouts  2.7 us (6%)
    pallas_call x1, Pallas kernels, mixing(): pl.pallas_call(functools.partial(mixing_body, wide, narrow, chunks), out_...  36.4 us
    pallas_call x1, Pallas kernels, gather_tokens(): pl.pallas_call(gather_body, out_shape=jax.ShapeDtypeStruct((rows * length...  9.05 us
    unnamed x5, local copies, waits for them, and re-layouts  2.7 us

profile of v5, /device:TPU:1, one launch (start us, length us, event | category | flops | bytes accessed | tf_op | source)
XLA Modules:
  0.0 48.1 jit_solution(2500973867300188231)
XLA Ops:
  0.0 0.0 copy-start.1
  0.0 0.7 %copy-done.1 = s32[1,8,16]{2,1,0:T(8,128)S(1)} copy-done((s32[1,8,16]{2,1,0:T(8,128)S(1)}, s32[1,8,16]{2,1,0:T(8,128)}, u32[]{:S(2)}) %copy-start.1) | copy-done | bytes 536
  0.7 9.1 %pick_tokens.1.local_ref = bf16[128,512]{1,0:T(8,128)(2,1)S(1)} custom-call(s32[1,8,16]{2,1,0:T(8,128)S(1)} %copy-done.1, bf16[512,32768]{1,0:T(8,128)(2,1)} %table_ref.1), custom_call_target="tpu_custom_call" | custom-call | tf_op jit(solution)/shard_map/pick_tokens/pallas_call | solution.py:177
  9.8 0.0 copy-start
  9.8 0.6 %copy-done = bf16[128,512]{1,0:T(8,128)(2,1)} copy-done((bf16[128,512]{1,0:T(8,128)(2,1)}, bf16[128,512]{1,0:T(8,128)(2,1)S(1)}, u32[]{:S(2)}) %copy-start) | copy-done | bytes 131096
  10.4 36.4 %mix_and_generate.1 = bf16[2,1,4,2048]{3,2,1,0:T(4,128)(2,1)} custom-call(bf16[128,512]{1,0:T(8,128)(2,1)} %copy-done, bf16[192,4096]{1,0:T(8,128)(2,1)} %bitcast.6, f32[1,4096]{1,0:T(1,128)} %bitcast.8, bf16[2,1,4,2048]{3,2,1,0:T(4,128)(2,1)} %refs_2_.1, bf16[2,1,4,2048]{3,2,1,0:T(4,128)(2,1)} %refs_3_.1, bf16[192,4096]{1,0:T(8,128)(2,1)} %bitcast.7, ...), custom_call_target="tpu_custom_call" | custom-call | tf_op jit(solution)/shard_map/mix_and_generate/pallas_call | solution.py:657
  46.8 1.4 %copy.22 = bf16[2,1,4,2048]{3,2,1,0:T(4,128)(2,1)} copy(bf16[2,1,4,2048]{3,2,1,0:T(4,128)(2,1)} %mix_and_generate.1) | data formatting | bytes 65536
Async XLA Ops:
  0.0 0.7 %copy-start.1 = (s32[1,8,16]{2,1,0:T(8,128)S(1)}, s32[1,8,16]{2,1,0:T(8,128)}, u32[]{:S(2)}) copy-start(s32[1,8,16]{2,1,0:T(8,128)} %ids_ref.1) | copy-start | bytes 1540
  9.8 0.6 %copy-start = (bf16[128,512]{1,0:T(8,128)(2,1)}, bf16[128,512]{1,0:T(8,128)(2,1)S(1)}, u32[]{:S(2)}) copy-start(bf16[128,512]{1,0:T(8,128)(2,1)S(1)} %pick_tokens.1.local_ref) | copy-start | bytes 393220

commit v6 on v5

--- a/solution.py
+++ b/solution.py
@@ -186,7 +186,7 @@
             pltpu.VMEM((rows, columns, length * lane_count), jnp.bfloat16),
             pltpu.SemaphoreType.DMA((rows, length)),
         ],
-        compiler_params=pltpu.CompilerParams(vmem_limit_bytes=40 * 2**20),
+        compiler_params=pltpu.CompilerParams(vmem_limit_bytes=24 * 2**20),
         name="pick_tokens",
     )(ids, table)
 
@@ -689,7 +689,7 @@
             dma((banks, share)),
         ],
         compiler_params=pltpu.CompilerParams(
-            collective_id=0, has_side_effects=True, vmem_limit_bytes=54 * 2**20
+            collective_id=0, has_side_effects=True, vmem_limit_bytes=52 * 2**20
         ),
         name="mix_and_generate",
     )(local, *operands)

time: 48.4 us -> 45.8 us (0.946)
  Pallas kernels: 45.4 us -> 44 us
  local copies, waits for them, and re-layouts: 2.7 us -> 1.36 us
    pallas_call x1, Pallas kernels: 36.4 us -> 35 us  [mixing(): pl.pallas_call(functools.partial(mixing_body, wide, narrow, chunks), out_...]
    unnamed x5 -> x31, local copies, waits for them, and re-layouts: 2.7 us -> 1.36 us
where the time goes in v6:
time: 45.8 us; the launch traced here: 45.6 us
  Pallas kernels  44 us (96%)
  local copies, waits for them, and re-layouts  1.36 us (3%)
    pallas_call x1, Pallas kernels, mixing(): pl.pallas_call(functools.partial(mixing_body, wide, narrow, chunks), out_...  35 us
    pallas_call x1, Pallas kernels, gather_tokens(): pl.pallas_call(gather_body, out_shape=jax.ShapeDtypeStruct((rows * length...  9.06 us
    unnamed x31, local copies, waits for them, and re-layouts  1.36 us

profile of v6, /device:TPU:1, one launch (start us, length us, event | category | flops | bytes accessed | tf_op | source)
XLA Modules:
  0.0 45.6 jit_solution(4041324159353383558)
XLA Ops:
  0.0 0.0 copy-start.12
  0.0 0.7 %copy-done.12 = s32[1,8,16]{2,1,0:T(8,128)S(1)} copy-done((s32[1,8,16]{2,1,0:T(8,128)S(1)}, s32[1,8,16]{2,1,0:T(8,128)}, u32[]{:S(2)}) %copy-start.12) | copy-done | bytes 536
  0.7 0.0 copy-start
  0.7 0.0 copy-start.1
  0.7 0.0 copy-start.2
  0.7 0.0 copy-start.4
  0.7 0.0 copy-start.5
  0.7 0.0 copy-start.6
  0.7 0.0 copy-start.7
  0.7 0.0 copy-start.8
  0.7 0.0 copy-start.9
  0.8 0.0 copy-start.10
  0.8 0.0 copy-start.11
  0.8 0.0 copy-start.13
  0.8 0.0 copy-start.14
  0.8 9.1 %pick_tokens.1.local_ref = bf16[128,512]{1,0:T(8,128)(2,1)S(1)} custom-call(s32[1,8,16]{2,1,0:T(8,128)S(1)} %copy-done.12, bf16[512,32768]{1,0:T(8,128)(2,1)} %table_ref.1), custom_call_target="tpu_custom_call" | custom-call | tf_op jit(solution)/shard_map/pick_tokens/pallas_call | solution.py:177
  9.9 0.0 copy-done
  9.9 0.0 copy-done.1
  9.9 0.0 copy-done.2
  9.9 0.0 copy-done.3
  9.9 0.0 copy-done.4
  9.9 0.0 copy-done.5
  9.9 0.0 copy-done.6
  9.9 0.0 copy-done.7
  9.9 0.0 copy-done.8
  10.0 0.0 copy-done.9
  10.0 0.0 copy-done.10
  10.0 0.0 copy-done.11
  10.0 0.0 copy-done.13
  10.0 0.0 copy-done.14
  10.0 35.0 %mix_and_generate.1 = bf16[2,1,4,2048]{3,2,1,0:T(4,128)(2,1)S(1)} custom-call(bf16[128,512]{1,0:T(8,128)(2,1)S(1)} %pick_tokens.1.local_ref, bf16[192,4096]{1,0:T(8,128)(2,1)} %bitcast.10, f32[1,4096]{1,0:T(1,128)S(1)} %bitcast.6, bf16[2,1,4,2048]{3,2,1,0:T(4,128)(2,1)S(1)} %copy-done.3, bf16[2,1,4,2048]{3,2,1,0:T(4,128)(2,1)S(1)} %copy-done.4, ...), custom_call_target="tpu_custom_call" | custom-call | tf_op jit(solution)/shard_map/mix_and_generate/pallas_call | solution.py:657
  45.0 0.6 %copy.22 = bf16[2,1,4,2048]{3,2,1,0:T(4,128)(2,1)} copy(bf16[2,1,4,2048]{3,2,1,0:T(4,128)(2,1)S(1)} %mix_and_generate.1) | data formatting | bytes 65536
  (1 shorter events, 0.0 us)
Async XLA Ops:
  0.0 0.7 %copy-start.12 = (s32[1,8,16]{2,1,0:T(8,128)S(1)}, s32[1,8,16]{2,1,0:T(8,128)}, u32[]{:S(2)}) copy-start(s32[1,8,16]{2,1,0:T(8,128)} %ids_ref.1) | copy-start | bytes 1540
  0.7 9.2 %copy-start = (bf16[4096,128]{1,0:T(8,128)(2,1)S(1)}, bf16[4096,128]{1,0:T(8,128)(2,1)}, u32[]{:S(2)}) copy-start(bf16[4096,128]{1,0:T(8,128)(2,1)} %refs_6_.1) | copy-start | bytes 3145732
  0.7 9.2 %copy-start.1 = (bf16[128,512]{1,0:T(8,128)(2,1)S(1)}, bf16[128,512]{1,0:T(8,128)(2,1)}, u32[]{:S(2)}) copy-start(bf16[128,512]{1,0:T(8,128)(2,1)} %refs_10_.1) | copy-start | bytes 393220
  0.7 9.2 %copy-start.2 = (f32[3,4096]{1,0:T(4,128)S(1)}, f32[3,4096]{1,0:T(4,128)}, u32[]{:S(2)}) copy-start(f32[3,4096]{1,0:T(4,128)} %refs_5_.1) | copy-start | bytes 147460
  0.7 9.2 %copy-start.3 = (bf16[2,1,4,2048]{3,2,1,0:T(4,128)(2,1)S(1)}, bf16[2,1,4,2048]{3,2,1,0:T(4,128)(2,1)}, u32[]{:S(2)}) copy-start(bf16[2,1,4,2048]{3,2,1,0:T(4,128)(2,1)} %refs_2_.1) | copy-start | bytes 98308
  0.7 9.2 %copy-start.4 = (bf16[2,1,4,2048]{3,2,1,0:T(4,128)(2,1)S(1)}, bf16[2,1,4,2048]{3,2,1,0:T(4,128)(2,1)}, u32[]{:S(2)}) copy-start(bf16[2,1,4,2048]{3,2,1,0:T(4,128)(2,1)} %refs_3_.1) | copy-start | bytes 98308
  0.7 9.2 %copy-start.5 = (bf16[2,1,4,2048]{3,2,1,0:T(4,128)(2,1)S(1)}, bf16[2,1,4,2048]{3,2,1,0:T(4,128)(2,1)}, u32[]{:S(2)}) copy-start(bf16[2,1,4,2048]{3,2,1,0:T(4,128)(2,1)} %refs_12_.1) | copy-start | bytes 98308
  0.7 9.2 %copy-start.6 = (bf16[2,1,4,2048]{3,2,1,0:T(4,128)(2,1)S(1)}, bf16[2,1,4,2048]{3,2,1,0:T(4,128)(2,1)}, u32[]{:S(2)}) copy-start(bf16[2,1,4,2048]{3,2,1,0:T(4,128)(2,1)} %refs_13_.1) | copy-start | bytes 98308
  0.7 9.2 %copy-start.7 = (bf16[2,1,4,2048]{3,2,1,0:T(4,128)(2,1)S(1)}, bf16[2,1,4,2048]{3,2,1,0:T(4,128)(2,1)}, u32[]{:S(2)}) copy-start(bf16[2,1,4,2048]{3,2,1,0:T(4,128)(2,1)} %refs_14_.1) | copy-start | bytes 98308
  0.7 9.2 %copy-start.8 = (f32[64,64]{1,0:T(8,128)S(1)}, f32[64,64]{1,0:T(8,128)}, u32[]{:S(2)}) copy-start(f32[64,64]{1,0:T(8,128)} %refs_15_.1) | copy-start | bytes 49156
  0.7 9.2 %copy-start.9 = (f32[4096]{0:T(1024)S(1)}, f32[4096]{0:T(1024)}, u32[]{:S(2)}) copy-start(f32[4096]{0:T(1024)} %param.23) | copy-start | bytes 49156
  0.8 9.2 %copy-start.10 = (f32[4096]{0:T(1024)S(1)}, f32[4096]{0:T(1024)}, u32[]{:S(2)}) copy-start(f32[4096]{0:T(1024)} %param.33) | copy-start | bytes 49156
  0.8 9.2 %copy-start.11 = (f32[4096]{0:T(1024)S(1)}, f32[4096]{0:T(1024)}, u32[]{:S(2)}) copy-start(f32[4096]{0:T(1024)} %param.34) | copy-start | bytes 49156
  0.8 9.2 %copy-start.13 = (f32[512]{0:T(512)S(1)}, f32[512]{0:T(512)}, u32[]{:S(2)}) copy-start(f32[512]{0:T(512)} %param.27) | copy-start | bytes 6148
  0.8 9.2 %copy-start.14 = (s32[1,8]{1,0:T(1,128)S(1)}, s32[1,8]{1,0:T(1,128)}, u32[]{:S(2)}) copy-start(s32[1,8]{1,0:T(1,128)} %refs_11_.1) | copy-start | bytes 100
